TPU v7x, 256 devices: a whole 4x4x8 slice. The times are simulated.
256 devices in a mesh: leaf: 32 (over z_hi, y, core), blk: 8 (over z_lo, x).
Axes of the slice: x: 4, y: 4, z: 8 (z_hi: 4, z_lo: 2; z = z_hi * 2 + z_lo), core: 2. Of those that a mesh axis runs over, the one named last changes fastest.
Arguments:
- sample: float32 [3, 229376, 512], P(None, ('leaf', 'blk')), may hold values from -6 to 6
- probes: float32 [3, 229376, 512], P(None, ('leaf', 'blk')), may hold values from -0.03125 to 0.03125
- skeleton_rows: int32 [14, 128], replicated, may hold values from 0 to 114687, as said below
Outputs:
- interpolants: float32 [3, 229376, 128], P(None, ('leaf', 'blk'))
- coupling: float32 [3, 32, 128, 128], P(None, 'leaf')
Inputs may be any that keep to these rules, and one draw needn't show every extreme that they name: `skeleton_rows`: list 2^(l+1) - 2 + j belongs to node j of level l; it holds 128 distinct row indices counted from the node's first row, below 229376 / 2^(l+1); its first entry is always 0 and its last entry is always the node's last row.
All inputs are finite; a program needn't handle non-finite values.
Results may differ from a plain program's by a relative error of at most 0.0003.
Values sent between devices are 32-bit elements; how exact they have to be, the bound alone decides.
A program may use at most 128 MiB of HBM per device.

v0:
```python
import jax
import jax.numpy as jnp
from jax import lax
from jax.sharding import PartitionSpec as P

ridge_term = 0.05


def partner_2(block, axis, bit):
    count = lax.axis_size(axis)
    route = []
    for low in range(count):
        high = low | 1 << bit
        if high != low and high < count:
            route += [(low, high), (high, low)]
    return lax.ppermute(block, axis, route)


def exact_dot(left_side, right_side):
    return jnp.dot(
        left_side, right_side, precision=lax.Precision.HIGHEST, preferred_element_type=jnp.float32
    )


def cross_rows(left_side, right_side):
    return lax.dot_general(
        left_side,
        right_side,
        (((1,), (1,)), ((), ())),
        precision=lax.Precision.HIGHEST,
        preferred_element_type=jnp.float32,
    )


def over_rows(left_side, right_side):
    return lax.dot_general(
        left_side,
        right_side,
        (((0,), (0,)), ((), ())),
        precision=lax.Precision.HIGHEST,
        preferred_element_type=jnp.float32,
    )


def chol_solve(gram_matrix, right_side):
    factor = jnp.linalg.cholesky(gram_matrix)
    return jax.scipy.linalg.cho_solve((factor, True), right_side)


def node_sum(local_term, split_bit):
    running = lax.psum(local_term, "blk")
    for bit_number in range(split_bit):
        running = running + partner_2(running, "leaf", bit_number)
    return running


def sibling_of(running, split_bit):
    return partner_2(running, "leaf", split_bit)


def local(sample, probes, skeleton_rows):
    levels, row_count, samples = sample.shape
    skel_count = skeleton_rows.shape[1]
    leaves = lax.axis_size("leaf")
    blocks = lax.axis_size("blk")
    tree_depth = leaves.bit_length() - 1
    leaf_index = lax.axis_index("leaf")
    blk_index = lax.axis_index("blk")
    first_row = (leaf_index * blocks + blk_index) * row_count
    row_total = row_count * leaves * blocks
    identity = jnp.eye(skel_count, dtype=jnp.float32)
    bases = []
    couplings = []
    for level_id in range(levels):
        split_bit = tree_depth - 1 - level_id
        node_id = leaf_index >> split_bit
        parity = node_id & 1
        node_rows = row_total >> level_id + 1
        current = sample[level_id]
        tests = probes[level_id]
        picked = lax.dynamic_index_in_dim(
            skeleton_rows, node_id + (2 ** (level_id + 1) - 2), 0, keepdims=False
        )
        local_pos = node_id * node_rows + picked - first_row
        owned_here = (local_pos >= 0) & (local_pos < row_count)
        safe_pos = jnp.clip(local_pos, 0, row_count - 1)
        corrections = []
        if level_id > 0:
            for coarse in range(level_id):
                coarse_bit = tree_depth - 1 - coarse
                local_term = over_rows(bases[coarse], tests)
                slot_ids = jnp.arange(2, dtype=jnp.int32)[:, None, None]
                parity_slots = jnp.where(slot_ids == parity, local_term[None], 0.0)
                sibling_sum = sibling_of(node_sum(parity_slots, coarse_bit), coarse_bit)
                chosen = lax.dynamic_index_in_dim(sibling_sum, 1 - parity, 0, keepdims=False)
                corrections.append(exact_dot(couplings[coarse], chosen))
        corrected = current
        for coarse in range(level_id):
            corrected = corrected - exact_dot(bases[coarse], corrections[coarse])
        taken_rows = jnp.where(owned_here[:, None], jnp.take(corrected, safe_pos, axis=0), 0.0)
        skeleton = node_sum(taken_rows, split_bit)
        gram_matrix = cross_rows(skeleton, skeleton) / samples + ridge_term * identity
        projected = cross_rows(corrected, skeleton) / samples
        basis_now = chol_solve(gram_matrix, projected.T).T
        bases.append(basis_now)
        moment = over_rows(basis_now, tests)
        partner = sibling_of(node_sum(moment, split_bit), split_bit)
        spread = cross_rows(partner, partner) + ridge_term * identity
        coupled = chol_solve(spread, cross_rows(partner, skeleton)).T
        couplings.append(coupled)
    return (jnp.stack(bases), jnp.stack(couplings)[:, None])


def solution(mesh):
    placed = (P(None, ("leaf", "blk"), None), P(None, ("leaf", "blk"), None), P())
    return jax.shard_map(
        local,
        mesh=mesh,
        in_specs=placed,
        out_specs=(P(None, ("leaf", "blk"), None), P(None, "leaf", None, None)),
        check_vma=False,
    )
```

profile of v0, /device:TPU:1, one launch (start us, length us, event | category | flops | bytes accessed | tf_op | source)
XLA Modules:
  0.0 971.9 jit_solution(17859655940000448337)
XLA Ops:
  11.4 78.0 %all-reduce.9.cloned.1.call-done = f32[128,512]{1,0:T(8,128)} async-done(((f32[128,512]{1,0:T(8,128)}), f32[128,512]{1,0:T(8,128)}) %all-reduce.9.cloned.1.call-update) | async-done | bytes 262160 | tf_op jit(solution)/shard_map/psum | solution.py:51
  98.6 6.3 collective-permute-done.1
  115.9 12.4 %collective-permute-done.3 = f32[128,512]{1,0:T(8,128)S(1)} collective-permute-done((f32[128,512]{1,0:T(8,128)S(1)}, f32[128,512]{1,0:T(8,128)S(1)}, u32[]{:S(2)}, u32[]{:S(2)}) %collective-permute-start.3) | collective-permute-done | bytes 262176 | tf_op jit(solution)/shard_map/ppermute | solution.py:16
  132.2 11.7 %cholesky.104 = f32[128,128]{1,0:T(8,128)S(1)} custom-call(f32[128,128]{1,0:T(8,128)S(1)} %fusion.65), custom_call_target="Cholesky" | custom-call | tf_op jit(solution)/shard_map/jit(cholesky)/cholesky | solution.py:46
  145.3 9.8 %custom-call.16 = f32[1,128,128]{1,2,0:T(8,128)S(1)} custom-call(f32[1,128,128]{2,1,0:T(8,128)S(1)} %fusion.31), custom_call_target="InvertDiagBlocksLowerTriangular" | custom-call | tf_op jit(solution)/shard_map/jit(_cho_solve)/triangular_solve | solution.py:47
  163.4 75.8 %all-reduce.19.cloned.1.call-done = (f32[128,512]{1,0:T(8,128)}, f32[2,128,512]{2,1,0:T(8,128)}) async-done(((f32[128,512]{1,0:T(8,128)}, f32[2,128,512]{2,1,0:T(8,128)}), (f32[128,512]{1,0:T(8,128)}, f32[2,128,512]{2,1,0:T(8,128)})) %all-reduce.19.cloned.1.call-update) | async-done | bytes 786448 | tf_op jit(solution)/shard_map/psum | solution.py:51
  244.7 11.2 %collective-permute-start.9 = (f32[2,128,512]{2,1,0:T(8,128)}, f32[2,128,512]{2,1,0:T(8,128)S(1)}, u32[]{:S(2)}, u32[]{:S(2)}) collective-permute-start(f32[2,128,512]{2,1,0:T(8,128)} %get-tuple-element.12), channel_id=1, source_target_pairs={{0,8},{8,0},{16,24},{24,16},{32,40},{40,32},{48,56},{56,48},{64,72... | collective-permute-start | bytes 1572872 | tf_op jit(solution)/shard_map/ppermute | solution.py:16
  274.9 10.7 %collective-permute-done.7 = f32[128,512]{1,0:T(8,128)S(1)} collective-permute-done((f32[128,512]{1,0:T(8,128)S(1)}, f32[128,512]{1,0:T(8,128)S(1)}, u32[]{:S(2)}, u32[]{:S(2)}) %collective-permute-start.7) | collective-permute-done | bytes 262176 | tf_op jit(solution)/shard_map/ppermute | solution.py:16
  293.3 8.6 collective-permute-done.8
  303.1 11.7 %cholesky.115 = f32[128,128]{1,0:T(8,128)S(1)} custom-call(f32[128,128]{1,0:T(8,128)S(1)} %fusion.60), custom_call_target="Cholesky" | custom-call | tf_op jit(solution)/shard_map/jit(cholesky)/cholesky | solution.py:46
  315.9 12.8 %collective-permute-done.12 = f32[2,128,512]{2,1,0:T(8,128)S(1)} collective-permute-done((f32[2,128,512]{2,1,0:T(8,128)S(1)}, f32[2,128,512]{2,1,0:T(8,128)S(1)}, u32[]{:S(2)}, u32[]{:S(2)}) %collective-permute-start.12) | collective-permute-done | bytes 524320 | tf_op jit(solution)/shard_map/ppermute | solution.py:16
  331.5 9.8 %custom-call.17 = f32[1,128,128]{1,2,0:T(8,128)S(1)} custom-call(f32[1,128,128]{2,1,0:T(8,128)S(1)} %fusion.32), custom_call_target="InvertDiagBlocksLowerTriangular" | custom-call | tf_op jit(solution)/shard_map/jit(_cho_solve)/triangular_solve | solution.py:47
  341.8 14.9 %collective-permute-done.13 = f32[2,128,512]{2,1,0:T(8,128)S(1)} collective-permute-done((f32[2,128,512]{2,1,0:T(8,128)S(1)}, f32[2,128,512]{2,1,0:T(8,128)S(1)}, u32[]{:S(2)}, u32[]{:S(2)}) %collective-permute-start.13) | collective-permute-done | bytes 524320 | tf_op jit(solution)/shard_map/ppermute | solution.py:16
  361.9 70.6 %all-reduce.11.cloned.1.call-done = f32[128,512]{1,0:T(8,128)} async-done(((f32[128,512]{1,0:T(8,128)}), f32[128,512]{1,0:T(8,128)}) %all-reduce.11.cloned.1.call-update) | async-done | bytes 262160 | tf_op jit(solution)/shard_map/psum | solution.py:51
  459.2 11.7 %cholesky.126 = f32[128,128]{1,0:T(8,128)S(1)} custom-call(f32[128,128]{1,0:T(8,128)S(1)} %fusion.55), custom_call_target="Cholesky" | custom-call | tf_op jit(solution)/shard_map/jit(cholesky)/cholesky | solution.py:46
  472.3 9.8 %custom-call.18 = f32[1,128,128]{1,2,0:T(8,128)S(1)} custom-call(f32[1,128,128]{2,1,0:T(8,128)S(1)} %fusion.33), custom_call_target="InvertDiagBlocksLowerTriangular" | custom-call | tf_op jit(solution)/shard_map/jit(_cho_solve)/triangular_solve | solution.py:47
  490.8 80.0 %all-reduce.17.cloned.1.call-done = (f32[2,128,512]{2,1,0:T(8,128)}, f32[128,512]{1,0:T(8,128)}, f32[2,128,512]{2,1,0:T(8,128)}) async-done(((f32[2,128,512]{2,1,0:T(8,128)}, f32[128,512]{1,0:T(8,128)}, f32[2,128,512]{2,1,0:T(8,128)}), (f32[2,128,512]{2,1,0:T(8,128)}, f32[128,512]{1,0:T(8,128)}, f32[2,128,512]{2,1,0:T(8,128)})) %all-reduce.17.cloned.1.call-update) | async-done | bytes 1310736 | tf_op jit(solution)/shard_map/psum | solution.py:51
  579.7 6.3 collective-permute-done.23
  597.7 7.8 collective-permute-done.27
  607.5 9.4 collective-permute-done.18
  620.4 11.7 %cholesky.137 = f32[128,128]{1,0:T(8,128)S(1)} custom-call(f32[128,128]{1,0:T(8,128)S(1)} %fusion.50), custom_call_target="Cholesky" | custom-call | tf_op jit(solution)/shard_map/jit(cholesky)/cholesky | solution.py:46
  632.7 6.5 collective-permute-done.19
  645.6 9.8 %custom-call.19 = f32[1,128,128]{1,2,0:T(8,128)S(1)} custom-call(f32[1,128,128]{2,1,0:T(8,128)S(1)} %fusion.34), custom_call_target="InvertDiagBlocksLowerTriangular" | custom-call | tf_op jit(solution)/shard_map/jit(_cho_solve)/triangular_solve | solution.py:47
  655.4 21.1 %collective-permute-done.20 = f32[2,128,512]{2,1,0:T(8,128)S(1)} collective-permute-done((f32[2,128,512]{2,1,0:T(8,128)S(1)}, f32[2,128,512]{2,1,0:T(8,128)S(1)}, u32[]{:S(2)}, u32[]{:S(2)}) %collective-permute-start.20) | collective-permute-done | bytes 524320 | tf_op jit(solution)/shard_map/ppermute | solution.py:16
  681.0 18.3 %collective-permute-done.29 = f32[2,128,512]{2,1,0:T(8,128)} collective-permute-done((f32[2,128,512]{2,1,0:T(8,128)S(1)}, f32[2,128,512]{2,1,0:T(8,128)}, u32[]{:S(2)}, u32[]{:S(2)}) %collective-permute-start.29) | collective-permute-done | bytes 524320 | tf_op jit(solution)/shard_map/ppermute | solution.py:16
  707.7 84.8 %all-reduce.13.cloned.1.call-done = f32[128,512]{1,0:T(8,128)} async-done(((f32[128,512]{1,0:T(8,128)}), f32[128,512]{1,0:T(8,128)}) %all-reduce.13.cloned.1.call-update) | async-done | bytes 262160 | tf_op jit(solution)/shard_map/psum | solution.py:51
  802.2 6.3 collective-permute-done.31
  813.3 11.7 %cholesky.148 = f32[128,128]{1,0:T(8,128)S(1)} custom-call(f32[128,128]{1,0:T(8,128)S(1)} %fusion.45), custom_call_target="Cholesky" | custom-call | tf_op jit(solution)/shard_map/jit(cholesky)/cholesky | solution.py:46
  826.3 9.8 %custom-call.20 = f32[1,128,128]{1,2,0:T(8,128)S(1)} custom-call(f32[1,128,128]{2,1,0:T(8,128)S(1)} %fusion.35), custom_call_target="InvertDiagBlocksLowerTriangular" | custom-call | tf_op jit(solution)/shard_map/jit(_cho_solve)/triangular_solve | solution.py:47
  840.7 74.3 %all-reduce.15.cloned.1.call-done = f32[128,512]{1,0:T(8,128)} async-done(((f32[128,512]{1,0:T(8,128)}), f32[128,512]{1,0:T(8,128)}) %all-reduce.15.cloned.1.call-update) | async-done | bytes 262160 | tf_op jit(solution)/shard_map/psum | solution.py:51
  940.3 11.7 %cholesky.159 = f32[128,128]{1,0:T(8,128)S(1)} custom-call(f32[128,128]{1,0:T(8,128)S(1)} %fusion.40), custom_call_target="Cholesky" | custom-call | tf_op jit(solution)/shard_map/jit(cholesky)/cholesky | solution.py:46
  953.3 9.8 %custom-call.21 = f32[1,128,128]{1,2,0:T(8,128)S(1)} custom-call(f32[1,128,128]{2,1,0:T(8,128)S(1)} %fusion.36), custom_call_target="InvertDiagBlocksLowerTriangular" | custom-call | tf_op jit(solution)/shard_map/jit(_cho_solve)/triangular_solve | solution.py:47
  (205 shorter events, 211.8 us)
Async XLA Ops:
  7.2 82.2 %all-reduce.9.cloned.1.call-start = ((), (), s32[]{:S(2)}) async-start(), calls=%async_computation | async-start | bytes 524288 | tf_op jit(solution)/shard_map/psum | solution.py:51
  11.3 227.8 %all-reduce.19.cloned.1.call-start = ((), (), s32[]{:S(2)}) async-start(), calls=%async_computation.5 | async-start | bytes 1572864 | tf_op jit(solution)/shard_map/psum | solution.py:51
  97.3 7.6 collective-permute-start.1
  104.9 8.2 collective-permute-start.2
  113.2 15.1 %collective-permute-start.3 = (f32[128,512]{1,0:T(8,128)S(1)}, f32[128,512]{1,0:T(8,128)S(1)}, u32[]{:S(2)}, u32[]{:S(2)}) collective-permute-start(f32[128,512]{1,0:T(8,128)S(1)} %add.216), channel_id=1, source_target_pairs={{0,64},{64,0},{8,72},{72,8},{16,80},{80,16},{24,88},{88,24},{32,96... | collective-permute-start | bytes 786440 | tf_op jit(solution)/shard_map/ppermute | solution.py:16
  163.3 269.2 %all-reduce.11.cloned.1.call-start = ((), (), s32[]{:S(2)}) async-start(), calls=%async_computation.1 | async-start | bytes 524288 | tf_op jit(solution)/shard_map/psum | solution.py:51
  239.1 16.8 %collective-permute-start.4 = (f32[128,512]{1,0:T(8,128)}, f32[128,512]{1,0:T(8,128)S(1)}, u32[]{:S(2)}, u32[]{:S(2)}) collective-permute-start(f32[128,512]{1,0:T(8,128)} %get-tuple-element.11), channel_id=1, source_target_pairs={{0,8},{8,0},{16,24},{24,16},{32,40},{40,32},{48,56},{56,48},{64,72... | collective-permute-start | bytes 786440 | tf_op jit(solution)/shard_map/ppermute | solution.py:16
  244.7 22.6 %collective-permute-start.9 = (f32[2,128,512]{2,1,0:T(8,128)}, f32[2,128,512]{2,1,0:T(8,128)S(1)}, u32[]{:S(2)}, u32[]{:S(2)}) collective-permute-start(f32[2,128,512]{2,1,0:T(8,128)} %get-tuple-element.12), channel_id=1, source_target_pairs={{0,8},{8,0},{16,24},{24,16},{32,40},{40,32},{48,56},{56,48},{64,72... | collective-permute-start | bytes 1572872 | tf_op jit(solution)/shard_map/ppermute | solution.py:16
  264.4 8.1 collective-permute-start.6
  267.3 23.0 %collective-permute-start.10 = (f32[2,128,512]{2,1,0:T(8,128)S(1)}, f32[2,128,512]{2,1,0:T(8,128)S(1)}, u32[]{:S(2)}, u32[]{:S(2)}) collective-permute-start(f32[2,128,512]{2,1,0:T(8,128)S(1)} %add.228), channel_id=1, source_target_pairs={{0,16},{16,0},{8,24},{24,8},{32,48},{48,32},{40,56},{56,40},{64,80... | collective-permute-start | bytes 1572872 | tf_op jit(solution)/shard_map/ppermute | solution.py:16
  272.5 13.0 %collective-permute-start.7 = (f32[128,512]{1,0:T(8,128)S(1)}, f32[128,512]{1,0:T(8,128)S(1)}, u32[]{:S(2)}, u32[]{:S(2)}) collective-permute-start(f32[128,512]{1,0:T(8,128)S(1)} %add.225), channel_id=1, source_target_pairs={{0,64},{64,0},{8,72},{72,8},{16,80},{80,16},{24,88},{88,24},{32,96... | collective-permute-start | bytes 786440 | tf_op jit(solution)/shard_map/ppermute | solution.py:16
  285.6 16.2 %collective-permute-start.8 = (f32[128,512]{1,0:T(8,128)S(1)}, f32[128,512]{1,0:T(8,128)S(1)}, u32[]{:S(2)}, u32[]{:S(2)}) collective-permute-start(f32[128,512]{1,0:T(8,128)S(1)} %add.226), channel_id=1, source_target_pairs={{0,128},{128,0},{8,136},{136,8},{16,144},{144,16},{24,152},{152,24... | collective-permute-start | bytes 786440 | tf_op jit(solution)/shard_map/ppermute | solution.py:16
  290.4 12.5 %collective-permute-start.11 = (f32[2,128,512]{2,1,0:T(8,128)S(1)}, f32[2,128,512]{2,1,0:T(8,128)S(1)}, u32[]{:S(2)}, u32[]{:S(2)}) collective-permute-start(f32[2,128,512]{2,1,0:T(8,128)S(1)} %add.229), channel_id=1, source_target_pairs={{0,32},{32,0},{8,40},{40,8},{16,48},{48,16},{24,56},{56,24},{64,96... | collective-permute-start | bytes 1572872 | tf_op jit(solution)/shard_map/ppermute | solution.py:16
  303.0 25.6 %collective-permute-start.12 = (f32[2,128,512]{2,1,0:T(8,128)S(1)}, f32[2,128,512]{2,1,0:T(8,128)S(1)}, u32[]{:S(2)}, u32[]{:S(2)}) collective-permute-start(f32[2,128,512]{2,1,0:T(8,128)S(1)} %add.230), channel_id=1, source_target_pairs={{0,64},{64,0},{8,72},{72,8},{16,80},{80,16},{24,88},{88,24},{32,96... | collective-permute-start | bytes 1572872 | tf_op jit(solution)/shard_map/ppermute | solution.py:16
  328.7 28.0 %collective-permute-start.13 = (f32[2,128,512]{2,1,0:T(8,128)S(1)}, f32[2,128,512]{2,1,0:T(8,128)S(1)}, u32[]{:S(2)}, u32[]{:S(2)}) collective-permute-start(f32[2,128,512]{2,1,0:T(8,128)S(1)} %add.231), channel_id=1, source_target_pairs={{0,128},{128,0},{8,136},{136,8},{16,144},{144,16},{24,152},{152,24... | collective-permute-start | bytes 1572872 | tf_op jit(solution)/shard_map/ppermute | solution.py:16
  361.9 208.9 %all-reduce.17.cloned.1.call-start = ((), (), s32[]{:S(2)}) async-start(), calls=%async_computation.4 | async-start | bytes 2621440 | tf_op jit(solution)/shard_map/psum | solution.py:51
  448.1 8.6 collective-permute-start.16
  490.7 301.8 %all-reduce.13.cloned.1.call-start = ((), (), s32[]{:S(2)}) async-start(), calls=%async_computation.2 | async-start | bytes 524288 | tf_op jit(solution)/shard_map/psum | solution.py:51
  576.1 12.8 %collective-permute-start.26 = (f32[2,128,512]{2,1,0:T(8,128)}, f32[2,128,512]{2,1,0:T(8,128)S(1)}, u32[]{:S(2)}, u32[]{:S(2)}) collective-permute-start(f32[2,128,512]{2,1,0:T(8,128)} %get-tuple-element.10), channel_id=1, source_target_pairs={{0,8},{8,0},{16,24},{24,16},{32,40},{40,32},{48,56},{56,48},{64,72... | collective-permute-start | bytes 1572872 | tf_op jit(solution)/shard_map/ppermute | solution.py:16
  576.1 13.3 %collective-permute-start.17 = (f32[2,128,512]{2,1,0:T(8,128)}, f32[2,128,512]{2,1,0:T(8,128)S(1)}, u32[]{:S(2)}, u32[]{:S(2)}) collective-permute-start(f32[2,128,512]{2,1,0:T(8,128)} %get-tuple-element.8), channel_id=1, source_target_pairs={{0,8},{8,0},{16,24},{24,16},{32,40},{40,32},{48,56},{56,48},{64,72... | collective-permute-start | bytes 1572872 | tf_op jit(solution)/shard_map/ppermute | solution.py:16
  586.1 8.3 collective-permute-start.24
  589.0 16.6 %collective-permute-start.27 = (f32[2,128,512]{2,1,0:T(8,128)S(1)}, f32[2,128,512]{2,1,0:T(8,128)S(1)}, u32[]{:S(2)}, u32[]{:S(2)}) collective-permute-start(f32[2,128,512]{2,1,0:T(8,128)S(1)} %add.250), channel_id=1, source_target_pairs={{0,16},{16,0},{8,24},{24,8},{32,48},{48,32},{40,56},{56,40},{64,80... | collective-permute-start | bytes 1572872 | tf_op jit(solution)/shard_map/ppermute | solution.py:16
  589.5 27.4 %collective-permute-start.18 = (f32[2,128,512]{2,1,0:T(8,128)S(1)}, f32[2,128,512]{2,1,0:T(8,128)}, u32[]{:S(2)}, u32[]{:S(2)}) collective-permute-start(f32[2,128,512]{2,1,0:T(8,128)S(1)} %add.241), channel_id=1, source_target_pairs={{0,16},{16,0},{8,24},{24,8},{32,48},{48,32},{40,56},{56,40},{64,80... | collective-permute-start | bytes 1572872 | tf_op jit(solution)/shard_map/ppermute | solution.py:16
  595.4 24.5 %collective-permute-start.25 = (f32[128,512]{1,0:T(8,128)S(1)}, f32[128,512]{1,0:T(8,128)S(1)}, u32[]{:S(2)}, u32[]{:S(2)}) collective-permute-start(f32[128,512]{1,0:T(8,128)S(1)} %add.248), channel_id=1, source_target_pairs={{0,64},{64,0},{8,72},{72,8},{16,80},{80,16},{24,88},{88,24},{32,96... | collective-permute-start | bytes 786440 | tf_op jit(solution)/shard_map/ppermute | solution.py:16
  605.7 37.7 %collective-permute-start.28 = (f32[2,128,512]{2,1,0:T(8,128)S(1)}, f32[2,128,512]{2,1,0:T(8,128)}, u32[]{:S(2)}, u32[]{:S(2)}) collective-permute-start(f32[2,128,512]{2,1,0:T(8,128)S(1)} %add.251), channel_id=1, source_target_pairs={{0,32},{32,0},{8,40},{40,8},{16,48},{48,16},{24,56},{56,24},{64,96... | collective-permute-start | bytes 1572872 | tf_op jit(solution)/shard_map/ppermute | solution.py:16
  618.0 21.2 %collective-permute-start.19 = (f32[2,128,512]{2,1,0:T(8,128)S(1)}, f32[2,128,512]{2,1,0:T(8,128)S(1)}, u32[]{:S(2)}, u32[]{:S(2)}) collective-permute-start(f32[2,128,512]{2,1,0:T(8,128)S(1)} %add.242), channel_id=1, source_target_pairs={{0,32},{32,0},{8,40},{40,8},{16,48},{48,16},{24,56},{56,24},{64,96... | collective-permute-start | bytes 1572872 | tf_op jit(solution)/shard_map/ppermute | solution.py:16
  639.3 37.2 %collective-permute-start.20 = (f32[2,128,512]{2,1,0:T(8,128)S(1)}, f32[2,128,512]{2,1,0:T(8,128)S(1)}, u32[]{:S(2)}, u32[]{:S(2)}) collective-permute-start(f32[2,128,512]{2,1,0:T(8,128)S(1)} %add.243), channel_id=1, source_target_pairs={{0,64},{64,0},{8,72},{72,8},{16,80},{80,16},{24,88},{88,24},{32,96... | collective-permute-start | bytes 1572872 | tf_op jit(solution)/shard_map/ppermute | solution.py:16
  644.5 54.8 %collective-permute-start.29 = (f32[2,128,512]{2,1,0:T(8,128)S(1)}, f32[2,128,512]{2,1,0:T(8,128)}, u32[]{:S(2)}, u32[]{:S(2)}) collective-permute-start(f32[2,128,512]{2,1,0:T(8,128)S(1)} %add.252), channel_id=1, source_target_pairs={{0,64},{64,0},{8,72},{72,8},{16,80},{80,16},{24,88},{88,24},{32,96... | collective-permute-start | bytes 1572872 | tf_op jit(solution)/shard_map/ppermute | solution.py:16
  676.6 24.1 %collective-permute-start.21 = (f32[2,128,512]{2,1,0:T(8,128)S(1)}, f32[2,128,512]{2,1,0:T(8,128)S(1)}, u32[]{:S(2)}, u32[]{:S(2)}) collective-permute-start(f32[2,128,512]{2,1,0:T(8,128)S(1)} %add.244), channel_id=1, source_target_pairs={{0,128},{128,0},{8,136},{136,8},{16,144},{144,16},{24,152},{152,24... | collective-permute-start | bytes 1572872 | tf_op jit(solution)/shard_map/ppermute | solution.py:16
  707.7 207.3 %all-reduce.15.cloned.1.call-start = ((), (), s32[]{:S(2)}) async-start(), calls=%async_computation.3 | async-start | bytes 524288 | tf_op jit(solution)/shard_map/psum | solution.py:51
  800.5 8.0 collective-permute-start.31
  931.3 8.5 collective-permute-start.34
  (19 other events, 294.9 us)
Sparse Core Ops, SparseCore 0:
  11.4 77.8 all-reduce.8
  163.4 75.6 all-reduce.18
  362.0 70.4 all-reduce.10
  490.9 79.8 all-reduce.16
  707.8 84.6 all-reduce.12
  840.8 74.1 all-reduce.14
where the time goes:
time: 971 us; the launch traced here: 972 us
  waiting for transfers between devices  651 us (67%)
  other arithmetic  155 us (16%)
  starting transfers between devices  97.4 us (10%)
  matrix products  45.5 us (5%)
  between operations  15 us (2%)
    psum x6, waiting for transfers between devices, node_sum(): running = lax.psum(local_term, 'blk')  463 us
    ppermute x35, waiting for transfers between devices, partner_2(): return lax.ppermute(block, axis, route)  188 us
    ppermute x35, starting transfers between devices, partner_2(): return lax.ppermute(block, axis, route)  97.2 us
    another operation x18, other arithmetic, chol_solve(): factor = jnp.linalg.cholesky(gram_matrix)  74.4 us
    another operation x12, other arithmetic, chol_solve(): return jax.scipy.linalg.cho_solve((factor, True), right_side)  62.8 us
  transfers between devices with their start and end apart: 41, of which 33 were waited for; matrix products, arithmetic and copies ran while one was open for 6% of the time, Pallas kernels for 0%

commit v1 on v0

v1 whole, which is shorter than its diff:
```python
import functools

import jax
import jax.numpy as jnp
from jax import lax
from jax.experimental import pallas as pl
from jax.experimental.pallas import tpu as pltpu
from jax.sharding import PartitionSpec as P

MESH = pl.DeviceIdType.MESH
F32 = jnp.float32
BF16 = jnp.bfloat16
ROWS = 896
SAMPLES = 512
SKEL = 128
RIDGE = 0.05
NROWS = 229376

HOPS = (0, 1, 2, 1)


def hops_of(d):
    return HOPS[d & 3] + (d >> 2 & 1) + (d >> 4 & 1)


PEERS = tuple(sorted(range(1, 32), key=lambda d: -hops_of(d)))
ROWMAJOR = (((1,), (0,)), ((), ()))
TRANSPOSED = (((1,), (1,)), ((), ()))


def split(x):
    hi = x.astype(BF16)
    return hi, (x - hi.astype(F32)).astype(BF16)


def dot(a, b, dims=ROWMAJOR):
    return lax.dot_general(a, b, dims, preferred_element_type=F32)


def exact(a, b, dims=ROWMAJOR):
    return lax.dot_general(a, b, dims, precision=lax.Precision.HIGHEST, preferred_element_type=F32)


def inverse(a):
    lane = lax.broadcasted_iota(jnp.int32, (8, 128), 1)
    sub = lax.broadcasted_iota(jnp.int32, (8, 128), 0)
    lane_rest = lax.broadcasted_iota(jnp.int32, (120, 128), 1)

    def body(_, a):
        p = a[0:8]
        c = [jnp.broadcast_to(p[:, i : i + 1], (8, 128)) for i in range(8)]
        for i in range(8):
            d = 1.0 / jnp.broadcast_to(c[i][i : i + 1], (8, 128))
            m = jnp.where(sub == i, 1.0 - d, c[i] * d)
            row = jnp.where(lane == i, 1.0, jnp.broadcast_to(p[i : i + 1], (8, 128)))
            z = jnp.where(lane == i, jnp.where(sub == i, 1.0, 0.0), p)
            p = z - m * row
            for j in range(i + 1, 8):
                c[j] = c[j] - m * jnp.broadcast_to(c[j][i : i + 1], (8, 128))
        r = a[8:]
        n = jnp.where(lane_rest < 8, 0.0, r)
        for i in range(8):
            n = n - r[:, i : i + 1] * p[i : i + 1]
        return pltpu.roll(jnp.concatenate([n, p], 0), 120, 1)

    return lax.fori_loop(0, 16, body, a)


def with_ridge(a, ridge):
    i = lax.broadcasted_iota(jnp.int32, (SKEL, SKEL), 0)
    j = lax.broadcasted_iota(jnp.int32, (SKEL, SKEL), 1)
    return a + jnp.where(i == j, ridge, 0.0)


def blocks_to_matrix(full):
    return jnp.concatenate([full[8 * c : 8 * c + 8].reshape(SKEL, 128) for c in range(4)], axis=1)


def kernel(
    rows_ref, sample_ref, probes_ref, basis_out, coupling_out,
    samp0, samp1, samp2, prob, sh, sl, pth, ptl, yref, basis, coup,
    st_a0, rs_a0, ex_a0, fu_a0,
    st_a1, rs_a1, ex_a1, fu_a1,
    st_b0, rs_b0, ex_b0, fu_b0,
    st_c0, rs_c0, ex_c0, exy_c0, fu_c0,
    st_b1, rs_b1, ex_b1, fu_b1,
    st_b2, rs_b2, ex_b2, fu_b2,
    red_a0, red_a1, red_b0, red_c0, red_b1, red_b2,
    ssem, rsem, insem, outsem,
):
    samp = (samp0, samp1, samp2)
    leaf = lax.axis_index("leaf")
    blk = lax.axis_index("blk")
    n2 = leaf // 4
    g = (leaf % 4) * 8 + blk
    leaf_step = [(1 - 2 * ((leaf // (1 << k)) % 2)) * (1 << k) for k in range(5)]
    blk_step = [(1 - 2 * ((blk // (1 << k)) % 2)) * (1 << k) for k in range(3)]

    def peer(d):
        a, b = leaf, blk
        for k in range(3):
            if d >> k & 1:
                b = b + blk_step[k]
        for k in range(2):
            if d >> (3 + k) & 1:
                a = a + leaf_step[k]
        return a, b

    def node(d):
        a = leaf
        for k in range(3):
            if d >> k & 1:
                a = a + leaf_step[2 + k]
        return a, blk

    loads = []
    for l in range(3):
        loads.append(pltpu.make_async_copy(sample_ref.at[l], samp[l], insem.at[l]))
    for l in range(3):
        loads.append(pltpu.make_async_copy(probes_ref.at[l], prob.at[l], insem.at[3 + l]))
    for c in loads:
        c.start()

    barrier = pltpu.get_barrier_semaphore()
    for d in PEERS:
        pl.semaphore_signal(barrier, inc=1, device_id=peer(d), device_id_type=MESH)
    for d in range(1, 8):
        pl.semaphore_signal(barrier, inc=1, device_id=node(d), device_id_type=MESH)

    def wait_bytes(ref, sem):
        pltpu.make_async_copy(ref, ref, sem).wait()

    def send(src, dst, stage, to):
        pltpu.make_async_remote_copy(
            src_ref=src, dst_ref=dst, send_sem=ssem.at[stage], recv_sem=rsem.at[stage],
            device_id=to, device_id_type=MESH,
        ).start()

    def scatter(st, rs, stage):
        for d in PEERS:
            a, b = peer(d)
            send(st.at[(a % 4) * 8 + b], rs.at[d - 1], stage, (a, b))

    def scattered(st, rs, stage):
        wait_bytes(rs, rsem.at[stage])
        return st[g] + jnp.sum(rs[...], axis=0)

    def gather(fu, stage):
        for d in PEERS:
            send(fu.at[g], fu.at[g], stage, peer(d))

    def gathered(fu, stage):
        wait_bytes(fu.at[pl.ds(1, 31)], rsem.at[stage])

    def pick(level, base, table_row, source, put):
        def one(i, _):
            at = rows_ref[table_row, i] + base
            own = (at >= 0) & (at < ROWS)
            safe = jnp.clip(at, 0, ROWS - 1)
            put(i, jnp.where(own, source(safe), 0.0))
            return 0

        lax.fori_loop(0, SKEL, one, 0, unroll=8)

    def table(level):
        node_id = leaf // (1 << (4 - level))
        base = node_id * (NROWS >> (level + 1)) - (leaf * 8 + blk) * ROWS
        return node_id + (2 ** (level + 1) - 2), base

    def pick_sample(level, st, offset):
        row, base = table(level)

        def put(i, v):
            for c in range(4):
                st[8 * c + i // 16, pl.ds(offset + i % 16, 1), :] = v[:, 128 * c : 128 * c + 128]

        pick(level, base, row, lambda at: samp[level][pl.ds(at, 1), :], put)

    def pick_y(level, st, first, offset):
        row, base = table(level)

        def put(i, v):
            st[first + i // 8, pl.ds(offset + i % 8, 1), :] = v

        pick(level, base, row, lambda at: yref[pl.ds(at, 1), :], put)

    def split_sample(l):
        hi, lo = split(samp[l][...])
        sh[l] = hi
        sl[l] = lo

    def split_probes(l):
        for i in range(7):
            t = prob[l, 128 * i : 128 * i + 128, :].T
            hi, lo = split(t)
            pth[l, :, 128 * i : 128 * i + 128] = hi
            ptl[l, :, 128 * i : 128 * i + 128] = lo

    def project(l, s):
        hi, lo = split(s)
        both = dot(sh[l], jnp.concatenate([hi, lo], axis=0), TRANSPOSED)
        return both[:, :SKEL] + both[:, SKEL:] + dot(sl[l], hi, TRANSPOSED)

    def test(l, yh, ycat):
        both = dot(pth[l], ycat)
        return both[:, :SKEL] + both[:, SKEL:] + dot(ptl[l], yh)

    def thin(a, b, dims=ROWMAJOR):
        ah, al = split(a)
        bh, bl = split(b)
        return dot(ah, bh, dims) + dot(ah, bl, dims) + dot(al, bh, dims)

    loads[0].wait()
    pick_sample(0, st_a0, 0)
    pl.semaphore_wait(barrier, 38)
    scatter(st_a0, rs_a0, 0)
    loads[1].wait()
    pick_sample(1, st_a1, 0)
    loads[2].wait()
    pick_sample(2, st_a1, 16)
    scatter(st_a1, rs_a1, 3)
    split_sample(0)
    red_a0[...] = scattered(st_a0, rs_a0, 0)
    for d in (1, 2, 3):
        send(red_a0, ex_a0.at[d - 1], 1, node(d))
    for c in loads[3:]:
        c.wait()
    split_probes(0)
    wait_bytes(ex_a0, rsem.at[1])
    fu_a0[g] = red_a0[...] + jnp.sum(ex_a0[...], axis=0)
    gather(fu_a0, 2)
    red_a1[...] = scattered(st_a1, rs_a1, 3)
    send(red_a1.at[pl.ds(0, 16)], ex_a1, 4, node(1))
    split_probes(1)
    split_probes(2)
    wait_bytes(ex_a1, rsem.at[4])
    fu_a1[g, 0:16] = red_a1[0:16] + ex_a1[...]
    fu_a1[g, 16:32] = red_a1[16:32]
    gathered(fu_a0, 2)
    gather(fu_a1, 5)

    s0 = blocks_to_matrix(fu_a0)
    y = project(0, s0)
    yref[...] = y
    yh, yl = split(y)
    ycat = jnp.concatenate([yh, yl], axis=1)
    st_b0[...] = test(0, yh, ycat).reshape(32, 16, 128)
    scatter(st_b0, rs_b0, 6)
    st_c0[:, 0:16] = test(1, yh, ycat).reshape(32, 16, 128)
    st_c0[:, 16:32] = test(2, yh, ycat).reshape(32, 16, 128)
    pick_y(1, st_c0, 0, 32)
    pick_y(2, st_c0, 16, 32)
    scatter(st_c0, rs_c0, 9)
    g0 = inverse(with_ridge(exact(s0, s0, TRANSPOSED), SAMPLES * RIDGE))
    red_b0[...] = exact(scattered(st_b0, rs_b0, 6), g0)
    for d in (4, 5, 6, 7):
        send(red_b0, ex_b0.at[d - 4], 7, node(d))
    basis[0] = thin(yref[...], g0)
    pltpu.make_async_copy(basis.at[0], basis_out.at[0], outsem.at[0]).start()
    split_sample(1)
    wait_bytes(ex_b0, rsem.at[7])
    fu_b0[g] = jnp.sum(ex_b0[...], axis=0)
    gather(fu_b0, 8)
    red_c0[...] = exact(scattered(st_c0, rs_c0, 9), g0)
    send(red_c0.at[pl.ds(0, 16)], ex_c0.at[pl.ds(32, 16)], 10, node(6))
    send(red_c0.at[pl.ds(0, 32)], ex_c0.at[pl.ds(0, 32)], 10, node(7))
    send(red_c0.at[pl.ds(16, 16)], ex_c0.at[pl.ds(48, 16)], 10, node(5))
    send(red_c0.at[pl.ds(32, 8)], exy_c0, 11, node(1))
    split_sample(2)
    wait_bytes(ex_c0, rsem.at[10])
    wait_bytes(exy_c0, rsem.at[11])
    fu_c0[g, 0:32] = ex_c0[0:32] + ex_c0[32:64]
    fu_c0[g, 32:40] = red_c0[32:40] + jnp.where(g < 16, exy_c0[...], 0.0)
    gathered(fu_b0, 8)
    gather(fu_c0, 12)

    def couple(s, mt):
        m = mt.T
        spread = inverse(with_ridge(exact(m, m, TRANSPOSED), RIDGE))
        return exact(exact(s, mt), spread)

    c0 = couple(s0, fu_b0[...].reshape(SAMPLES, SKEL))
    coup[0] = c0

    gathered(fu_a1, 5)
    gathered(fu_c0, 12)
    r1 = blocks_to_matrix(fu_a1[:, 0:16])
    b01 = fu_c0[0:16, 32:40].reshape(SKEL, SKEL)
    k1t = exact(fu_c0[:, 0:16].reshape(SAMPLES, SKEL), c0, TRANSPOSED)
    s1 = r1 - exact(b01, k1t, TRANSPOSED)
    y = project(1, s1) - thin(basis[0], exact(s1, k1t), TRANSPOSED)
    yref[...] = y
    yh, yl = split(y)
    ycat = jnp.concatenate([yh, yl], axis=1)
    st_b1[:, 0:16] = test(1, yh, ycat).reshape(32, 16, 128)
    st_b1[:, 16:32] = test(2, yh, ycat).reshape(32, 16, 128)
    pick_y(2, st_b1, 0, 32)
    st_b1[16:32, 32:40] = jnp.zeros((16, 8, 128), F32)
    scatter(st_b1, rs_b1, 13)
    g1 = inverse(with_ridge(exact(s1, s1, TRANSPOSED), SAMPLES * RIDGE))
    red_b1[...] = exact(scattered(st_b1, rs_b1, 13), g1)
    send(red_b1.at[pl.ds(0, 32)], ex_b1.at[pl.ds(0, 32)], 14, node(3))
    send(red_b1.at[pl.ds(0, 16)], ex_b1.at[pl.ds(32, 16)], 14, node(2))
    basis[1] = thin(yref[...], g1)
    pltpu.make_async_copy(basis.at[1], basis_out.at[1], outsem.at[1]).start()
    b02 = fu_c0[16:32, 32:40].reshape(SKEL, SKEL)
    k2t = exact(fu_c0[:, 16:32].reshape(SAMPLES, SKEL), c0, TRANSPOSED)
    part2 = blocks_to_matrix(fu_a1[:, 16:32]) - exact(b02, k2t, TRANSPOSED)
    wait_bytes(ex_b1, rsem.at[14])
    fu_b1[g, 0:16] = ex_b1[0:16] + ex_b1[32:48]
    fu_b1[g, 16:32] = ex_b1[16:32]
    fu_b1[g, 32:40] = red_b1[32:40]
    gather(fu_b1, 15)
    gathered(fu_b1, 15)
    c1 = couple(s1, fu_b1[:, 0:16].reshape(SAMPLES, SKEL))
    coup[1] = c1

    b12 = fu_b1[0:16, 32:40].reshape(SKEL, SKEL)
    k3t = exact(fu_b1[:, 16:32].reshape(SAMPLES, SKEL), c1, TRANSPOSED)
    s2 = part2 - exact(b12, k3t, TRANSPOSED)
    y = project(2, s2) - thin(basis[0], exact(s2, k2t), TRANSPOSED) - thin(basis[1], exact(s2, k3t), TRANSPOSED)
    yref[...] = y
    yh, yl = split(y)
    ycat = jnp.concatenate([yh, yl], axis=1)
    st_b2[...] = test(2, yh, ycat).reshape(32, 16, 128)
    scatter(st_b2, rs_b2, 16)
    g2 = inverse(with_ridge(exact(s2, s2, TRANSPOSED), SAMPLES * RIDGE))
    red_b2[...] = exact(scattered(st_b2, rs_b2, 16), g2)
    send(red_b2, ex_b2, 17, node(1))
    basis[2] = thin(yref[...], g2)
    pltpu.make_async_copy(basis.at[2], basis_out.at[2], outsem.at[2]).start()
    wait_bytes(ex_b2, rsem.at[17])
    fu_b2[g] = ex_b2[...]
    gather(fu_b2, 18)
    gathered(fu_b2, 18)
    coup[2] = couple(s2, fu_b2[...].reshape(SAMPLES, SKEL))
    pltpu.make_async_copy(coup, coupling_out, outsem.at[3]).start()

    for rs, stage in ((rs_a0, 0), (rs_a1, 3), (rs_b0, 6), (rs_c0, 9), (rs_b1, 13), (rs_b2, 16)):
        wait_bytes(rs, ssem.at[stage])
    for fu, stage in ((fu_a0, 2), (fu_a1, 5), (fu_b0, 8), (fu_c0, 12), (fu_b1, 15), (fu_b2, 18)):
        wait_bytes(fu.at[pl.ds(1, 31)], ssem.at[stage])
    for ex, stage in ((ex_a0, 1), (ex_a1, 4), (ex_b0, 7), (ex_c0, 10), (exy_c0, 11), (ex_b1, 14), (ex_b2, 17)):
        wait_bytes(ex, ssem.at[stage])
    for l in range(3):
        pltpu.make_async_copy(basis.at[l], basis_out.at[l], outsem.at[l]).wait()
    pltpu.make_async_copy(coup, coupling_out, outsem.at[3]).wait()


def vm(*shape, dtype=F32):
    return pltpu.VMEM(shape, dtype)


def local(sample, probes, skeleton_rows):
    def quad(rows, ex):
        return [vm(32, rows, 128), vm(31, rows, 128)] + ex + [vm(32, rows, 128)]

    scratch = [
        vm(ROWS, SAMPLES), vm(ROWS, SAMPLES), vm(ROWS, SAMPLES), vm(3, ROWS, SAMPLES),
        vm(3, ROWS, SAMPLES, dtype=BF16), vm(3, ROWS, SAMPLES, dtype=BF16),
        vm(3, SAMPLES, ROWS, dtype=BF16), vm(3, SAMPLES, ROWS, dtype=BF16),
        vm(ROWS, SKEL), vm(3, ROWS, SKEL), vm(3, SKEL, SKEL),
        *quad(16, [vm(3, 16, 128)]),
        *quad(32, [vm(16, 128)]),
        *quad(16, [vm(4, 16, 128)]),
        *quad(40, [vm(64, 128), vm(8, 128)]),
        *quad(40, [vm(48, 128)]),
        *quad(16, [vm(16, 128)]),
        vm(16, 128), vm(32, 128), vm(16, 128), vm(40, 128), vm(40, 128), vm(16, 128),
        pltpu.SemaphoreType.DMA((19,)), pltpu.SemaphoreType.DMA((19,)),
        pltpu.SemaphoreType.DMA((6,)), pltpu.SemaphoreType.DMA((4,)),
    ]
    basis, coupling = pl.pallas_call(
        kernel,
        out_shape=(
            jax.ShapeDtypeStruct((3, ROWS, SKEL), F32),
            jax.ShapeDtypeStruct((3, SKEL, SKEL), F32),
        ),
        in_specs=[
            pl.BlockSpec(memory_space=pltpu.SMEM),
            pl.BlockSpec(memory_space=pl.ANY),
            pl.BlockSpec(memory_space=pl.ANY),
        ],
        out_specs=(pl.BlockSpec(memory_space=pl.ANY), pl.BlockSpec(memory_space=pl.ANY)),
        scratch_shapes=scratch,
        compiler_params=pltpu.CompilerParams(
            collective_id=0, has_side_effects=True, vmem_limit_bytes=52 * 2**20
        ),
    )(skeleton_rows, sample, probes)
    return basis, coupling[:, None]


def solution(mesh):
    placed = (P(None, ("leaf", "blk"), None), P(None, ("leaf", "blk"), None), P())
    return jax.shard_map(
        local,
        mesh=mesh,
        in_specs=placed,
        out_specs=(P(None, ("leaf", "blk"), None), P(None, "leaf", None, None)),
        check_vma=False,
    )
```

time: 971 us -> 129 us (0.13)
  waiting for transfers between devices: 651 us -> 0 us
  other arithmetic: 155 us -> 0 us
  Pallas kernels: 0 us -> 126 us
  starting transfers between devices: 97.4 us -> 0 us
  matrix products: 45.5 us -> 0 us
  between operations: 15 us -> 0.65 us
    psum x6 -> x0, waiting for transfers between devices: 463 us -> none  [node_sum(): running = lax.psum(local_term, 'blk')]
    ppermute x35 -> x0, waiting for transfers between devices: 188 us -> none  [partner_2(): return lax.ppermute(block, axis, route)]
    another operation x31 -> x0, other arithmetic: 137 us -> none  [the longest x18 74.4 us: chol_solve(): factor = jnp.linalg.cholesky(gram_matrix)]
    pallas_call x0 -> x1, Pallas kernels: none -> 126 us  [local(): pl.pallas_call(kernel, out_shape=(jax.ShapeDtypeStruct((3, ROWS, SKEL), F...]
    ppermute x35 -> x0, starting transfers between devices: 97.2 us -> none  [partner_2(): return lax.ppermute(block, axis, route)]
    dot_general x24 -> x0, matrix products: 40.8 us -> none  [the longest x6 18.6 us: over_rows(): lax.dot_general(left_side, right_side, (((0,), (0,)), ((), ())), precisio...]
    add x29 -> x0, other arithmetic: 11 us -> none  [node_sum(): running = running + partner_2(running, 'leaf', bit_number)]
  transfers between devices with their start and end apart: 41 -> 0, of which waited for: 33 -> 0; matrix products, arithmetic and copies ran while one was open for 6% -> 0% of each run, Pallas kernels for 0% -> 0%
where the time goes in v1:
time: 129 us
  Pallas kernels  126 us (98%)
  local copies, waits for them, and re-layouts  2.45 us (2%)
    pallas_call x1, Pallas kernels, local(): pl.pallas_call(kernel, out_shape=(jax.ShapeDtypeStruct((3, ROWS, SKEL), F...  126 us

profile of v1, /device:TPU:1, one launch (start us, length us, event | category | flops | bytes accessed | tf_op | source)
XLA Modules:
  0.0 128.7 jit_solution(653343039015741859)
XLA Ops:
  0.6 0.0 copy-start
  0.6 0.7 copy-done
  1.3 125.6 %shard_map.50 = (f32[3,896,128]{2,1,0:T(8,128)S(1)}, f32[3,128,128]{2,1,0:T(8,128)S(1)}) custom-call(s32[14,128]{1,0:T(8,128)S(1)} %copy-done, f32[3,896,512]{2,1,0:T(8,128)} %sample_ref.1, f32[3,896,512]{2,1,0:T(8,128)} %probes_ref.1), custom_call_target="tpu_custom_call" | custom-call | tf_op jit(solution)/shard_map/pallas_call | solution.py:373
  127.0 1.1 copy.8
  128.0 0.7 copy.9
Async XLA Ops:
  0.6 0.7 copy-start

commit v2 on v1

v2 whole, which is shorter than its diff:
```python
import functools

import jax
import jax.numpy as jnp
from jax import lax
from jax.experimental import pallas as pl
from jax.experimental.pallas import tpu as pltpu
from jax.sharding import PartitionSpec as P

MESH = pl.DeviceIdType.MESH
F32 = jnp.float32
BF16 = jnp.bfloat16
ROWS = 896
SAMPLES = 512
SKEL = 128
RIDGE = 0.05
NROWS = 229376

STEP = 16

HOPS = (0, 1, 2, 1)


def far(mask):
    a, b = mask
    return HOPS[a >> 1 & 3] + HOPS[b & 3] + (b >> 2)


def masks(first, leaf_bits, blk_bits):
    every = [(first + a, b) for a in range(1 << leaf_bits) for b in range(1 << blk_bits)]
    return tuple(sorted((m for m in every if m != (0, 0)), key=lambda m: -far(m)))


NODE = masks(0, 2, 3)
PLANE = masks(0, 3, 2)
SIBLING = masks(4, 2, 3)
HALF = ((0, 4), (8, 0), (8, 4))
ACROSS = ((16, 0), (16, 4), (24, 0), (24, 4))
OTHERS = HALF + ACROSS + ((20, 0), (28, 0), (12, 0))
ALL = tuple(dict.fromkeys(SIBLING + NODE + PLANE + OTHERS))

ROWMAJOR = (((1,), (0,)), ((), ()))
TRANSPOSED = (((1,), (1,)), ((), ()))


def split(x):
    hi = x.astype(BF16)
    return hi, (x - hi.astype(F32)).astype(BF16)


def dot(a, b, dims=ROWMAJOR):
    return lax.dot_general(a, b, dims, preferred_element_type=F32)


def exact(a, b, dims=ROWMAJOR):
    return lax.dot_general(a, b, dims, precision=lax.Precision.HIGHEST, preferred_element_type=F32)


def inverse(a):
    lane = lax.broadcasted_iota(jnp.int32, (STEP, 128), 1)
    sub = lax.broadcasted_iota(jnp.int32, (STEP, 128), 0)
    lane_rest = lax.broadcasted_iota(jnp.int32, (128 - STEP, 128), 1)

    def body(_, a):
        p = a[0:STEP]
        c = [jnp.broadcast_to(p[:, i : i + 1], (STEP, 128)) for i in range(STEP)]
        for i in range(STEP):
            d = 1.0 / jnp.broadcast_to(c[i][i : i + 1], (STEP, 128))
            m = jnp.where(sub == i, 1.0 - d, c[i] * d)
            row = jnp.where(lane == i, 1.0, jnp.broadcast_to(p[i : i + 1], (STEP, 128)))
            z = jnp.where(lane == i, jnp.where(sub == i, 1.0, 0.0), p)
            p = z - m * row
            for j in range(i + 1, STEP):
                c[j] = c[j] - m * jnp.broadcast_to(c[j][i : i + 1], (STEP, 128))
        r = a[STEP:]
        n = jnp.where(lane_rest < STEP, 0.0, r)
        for i in range(STEP):
            n = n - r[:, i : i + 1] * p[i : i + 1]
        return pltpu.roll(jnp.concatenate([n, p], 0), 128 - STEP, 1)

    return lax.fori_loop(0, 128 // STEP, body, a)


def with_ridge(a, ridge):
    i = lax.broadcasted_iota(jnp.int32, (SKEL, SKEL), 0)
    j = lax.broadcasted_iota(jnp.int32, (SKEL, SKEL), 1)
    return a + jnp.where(i == j, ridge, 0.0)


def blocks_to_matrix(full):
    return jnp.concatenate([full[8 * c : 8 * c + 8].reshape(SKEL, 128) for c in range(4)], axis=1)


def kernel(
    rows_ref, sample_ref, probes_ref, basis_out, coupling_out,
    samp0, samp1, samp2, prob, sh, sl, pth, ptl, yref, basis, coup,
    st_a0, rs_a0, ex_a0, fu_a0, red_a0,
    st_a1, rs_a1, ex_a1, fu_a1, red_a1,
    st_b0, rs_b0, ex_b0, fu_b0, red_b0,
    st_c0, rs_c0, ex_c0, exy_c0, fu_c0, red_c0,
    st_d0, rs_d0, ex_d0, fu_d0, red_d0,
    st_b1, rs_b1, ex_b1, fu_b1, red_b1,
    st_d1, rs_d1, ex_d1, fu_d1, red_d1,
    st_b2, rs_b2, ex_b2, fu_b2, red_b2,
    ssem, rsem, insem, outsem,
):
    samp = (samp0, samp1, samp2)
    leaf = lax.axis_index("leaf")
    blk = lax.axis_index("blk")
    leaf_step = [(1 - 2 * ((leaf // (1 << k)) % 2)) * (1 << k) for k in range(5)]
    blk_step = [(1 - 2 * ((blk // (1 << k)) % 2)) * (1 << k) for k in range(3)]

    def at(mask):
        a, b = leaf, blk
        for k in range(5):
            if mask[0] >> k & 1:
                a = a + leaf_step[k]
        for k in range(3):
            if mask[1] >> k & 1:
                b = b + blk_step[k]
        return a, b

    def in_node(a, b):
        return (a % 4) * 8 + b

    def in_plane(a, b):
        return (a % 8) * 4 + b % 4

    gn = in_node(leaf, blk)
    gp = in_plane(leaf, blk)

    loads = {}
    for l in range(3):
        loads[l] = pltpu.make_async_copy(sample_ref.at[l], samp[l], insem.at[l])
    for l in range(3):
        loads[3 + l] = pltpu.make_async_copy(probes_ref.at[l], prob.at[l], insem.at[3 + l])
    for c in loads.values():
        c.start()

    barrier = pltpu.get_barrier_semaphore()
    for m in ALL:
        pl.semaphore_signal(barrier, inc=1, device_id=at(m), device_id_type=MESH)

    leaving, landing, writing = [], {}, []

    def wait_bytes(ref, sem):
        pltpu.make_async_copy(ref, ref, sem).wait()

    def start(ref, stage):
        leaving.append((ref, stage))
        landing[stage] = ref

    def arrive(stage):
        wait_bytes(landing.pop(stage), rsem.at[stage])

    def write(src, dst, i):
        copy = pltpu.make_async_copy(src, dst, outsem.at[i])
        copy.start()
        writing.append(copy)

    def finish():
        for copy in loads.values():
            copy.wait()
        for stage in tuple(landing):
            arrive(stage)
        for ref, stage in leaving:
            wait_bytes(ref, ssem.at[stage])
        for copy in writing:
            copy.wait()

    def send(src, dst, stage, to):
        pltpu.make_async_remote_copy(
            src_ref=src, dst_ref=dst, send_sem=ssem.at[stage], recv_sem=rsem.at[stage],
            device_id=to, device_id_type=MESH,
        ).start()

    def scatter(st, rs, stage, group, number):
        for i, m in enumerate(group):
            to = at(m)
            send(st.at[number(*to)], rs.at[i], stage, to)
        start(rs, stage)

    def exchange(pieces, ex, stage):
        for src, dst, m in pieces:
            send(src, dst, stage, at(m))
        start(ex, stage)

    def gather(fu, stage, group, mine):
        for m in group:
            send(fu.at[mine], fu.at[mine], stage, at(m))
        start(fu.at[pl.ds(1, 31)], stage)

    def pick(level, base, table_row, source, put):
        def one(i, _):
            place = rows_ref[table_row, i] + base
            own = (place >= 0) & (place < ROWS)
            safe = jnp.clip(place, 0, ROWS - 1)
            put(i, jnp.where(own, source(safe), 0.0))
            return 0

        lax.fori_loop(0, SKEL, one, 0, unroll=8)

    def table(level):
        node_id = leaf // (1 << (4 - level))
        base = node_id * (NROWS >> (level + 1)) - (leaf * 8 + blk) * ROWS
        return node_id + (2 ** (level + 1) - 2), base

    def pick_sample(level, st, offset):
        row, base = table(level)

        def put(i, v):
            for c in range(4):
                st[8 * c + i // 16, pl.ds(offset + i % 16, 1), :] = v[:, 128 * c : 128 * c + 128]

        pick(level, base, row, lambda i: samp[level][pl.ds(i, 1), :], put)

    def pick_y(level, st, offset):
        row, base = table(level)

        def put(i, v):
            st[i // 8, pl.ds(offset + i % 8, 1), :] = v

        pick(level, base, row, lambda i: yref[pl.ds(i, 1), :], put)
        st[16:32, offset : offset + 8] = jnp.zeros((16, 8, 128), F32)

    def split_sample(l):
        hi, lo = split(samp[l][...])
        sh[l] = hi
        sl[l] = lo

    def split_probes(l):
        for i in range(7):
            t = prob[l, 128 * i : 128 * i + 128, :].T
            hi, lo = split(t)
            pth[l, :, 128 * i : 128 * i + 128] = hi
            ptl[l, :, 128 * i : 128 * i + 128] = lo

    def project(l, s):
        hi, lo = split(s)
        both = dot(sh[l], jnp.concatenate([hi, lo], axis=0), TRANSPOSED)
        return both[:, :SKEL] + both[:, SKEL:] + dot(sl[l], hi, TRANSPOSED)

    def test(l, yh, ycat):
        both = dot(pth[l], ycat)
        return both[:, :SKEL] + both[:, SKEL:] + dot(ptl[l], yh)

    def thin(a, b, dims=ROWMAJOR):
        ah, al = split(a)
        bh, bl = split(b)
        return dot(ah, bh, dims) + dot(ah, bl, dims) + dot(al, bh, dims)

    def couple(s, mt):
        m = mt.T
        spread = inverse(with_ridge(exact(m, m, TRANSPOSED), RIDGE))
        return exact(exact(s, mt), spread)

    def gram_inverse(s):
        return inverse(with_ridge(exact(s, s, TRANSPOSED), SAMPLES * RIDGE))

    loads.pop(0).wait()
    pick_sample(0, st_a0, 0)
    pl.semaphore_wait(barrier, len(ALL))
    scatter(st_a0, rs_a0, 0, PLANE, in_plane)
    loads.pop(1).wait()
    pick_sample(1, st_a1, 0)
    scatter(st_a1, rs_a1, 3, PLANE, in_plane)
    split_sample(0)
    arrive(0)
    red_a0[...] = st_a0[gp] + jnp.sum(rs_a0[...], axis=0)
    exchange([(red_a0, ex_a0.at[i], m) for i, m in enumerate(HALF)], ex_a0, 1)
    loads.pop(3).wait()
    split_probes(0)
    arrive(3)
    red_a1[...] = st_a1[gp] + jnp.sum(rs_a1[...], axis=0)
    arrive(1)
    fu_a0[gp] = red_a0[...] + jnp.sum(ex_a0[...], axis=0)
    gather(fu_a0, 2, PLANE, gp)
    exchange([(red_a1, ex_a1, (0, 4))], ex_a1, 4)
    loads.pop(2).wait()
    pick_sample(2, st_d0, 24)
    loads.pop(4).wait()
    split_probes(1)
    loads.pop(5).wait()
    split_probes(2)
    arrive(4)
    fu_a1[gp] = red_a1[...] + ex_a1[...]
    gather(fu_a1, 5, PLANE, gp)

    arrive(2)
    s0 = blocks_to_matrix(fu_a0)
    y = project(0, s0)
    yref[...] = y
    yh, yl = split(y)
    ycat = jnp.concatenate([yh, yl], axis=1)
    st_b0[...] = test(0, yh, ycat).reshape(32, 16, 128)
    scatter(st_b0, rs_b0, 6, PLANE, in_plane)
    st_c0[:, 0:16] = test(1, yh, ycat).reshape(32, 16, 128)
    pick_y(1, st_c0, 16)
    scatter(st_c0, rs_c0, 9, PLANE, in_plane)
    g0 = gram_inverse(s0)
    arrive(6)
    red_b0[...] = exact(st_b0[gp] + jnp.sum(rs_b0[...], axis=0), g0)
    exchange([(red_b0, ex_b0.at[i], m) for i, m in enumerate(ACROSS)], ex_b0, 7)
    arrive(9)
    red_c0[...] = exact(st_c0[gp] + jnp.sum(rs_c0[...], axis=0), g0)
    exchange([(red_c0.at[pl.ds(0, 16)], ex_c0.at[i], m) for i, m in enumerate(ACROSS[2:])], ex_c0, 10)
    exchange([(red_c0.at[pl.ds(16, 8)], exy_c0, (0, 4))], exy_c0, 11)
    st_d0[:, 0:16] = test(2, yh, ycat).reshape(32, 16, 128)
    pick_y(2, st_d0, 16)
    arrive(7)
    fu_b0[gp] = jnp.sum(ex_b0[...], axis=0)
    gather(fu_b0, 8, PLANE, gp)
    arrive(10)
    arrive(11)
    fu_c0[gp, 0:16] = jnp.sum(ex_c0[...], axis=0)
    fu_c0[gp, 16:24] = red_c0[16:24] + exy_c0[...]
    gather(fu_c0, 12, PLANE, gp)
    basis[0] = thin(yref[...], g0)
    write(basis.at[0], basis_out.at[0], 0)
    split_sample(1)
    arrive(8)
    scatter(st_d0, rs_d0, 13, NODE, in_node)
    c0 = couple(s0, fu_b0[...].reshape(SAMPLES, SKEL))
    coup[0] = c0

    arrive(5)
    arrive(12)
    k1t = exact(fu_c0[:, 0:16].reshape(SAMPLES, SKEL), c0, TRANSPOSED)
    s1 = blocks_to_matrix(fu_a1) - exact(fu_c0[0:16, 16:24].reshape(SKEL, SKEL), k1t, TRANSPOSED)
    y = project(1, s1) - thin(basis[0], exact(s1, k1t), TRANSPOSED)
    yref[...] = y
    yh, yl = split(y)
    ycat = jnp.concatenate([yh, yl], axis=1)
    st_b1[...] = test(1, yh, ycat).reshape(32, 16, 128)
    scatter(st_b1, rs_b1, 16, PLANE, in_plane)
    st_d1[:, 0:16] = test(2, yh, ycat).reshape(32, 16, 128)
    pick_y(2, st_d1, 16)
    scatter(st_d1, rs_d1, 19, NODE, in_node)
    arrive(13)
    sum_d0 = st_d0[gn] + jnp.sum(rs_d0[...], axis=0)
    red_d0[0:24] = exact(sum_d0[0:24], g0)
    red_d0[24:40] = sum_d0[24:40]
    exchange([(red_d0.at[pl.ds(0, 16)], ex_d0.at[i], m) for i, m in enumerate(((20, 0), (28, 0)))], ex_d0, 14)
    g1 = gram_inverse(s1)
    arrive(16)
    red_b1[...] = exact(st_b1[gp] + jnp.sum(rs_b1[...], axis=0), g1)
    exchange([(red_b1, ex_b1.at[i], m) for i, m in enumerate(((8, 0), (8, 4)))], ex_b1, 17)
    arrive(19)
    red_d1[...] = exact(st_d1[gn] + jnp.sum(rs_d1[...], axis=0), g1)
    exchange([(red_d1.at[pl.ds(0, 16)], ex_d1, (12, 0))], ex_d1, 20)
    arrive(17)
    fu_b1[gp] = jnp.sum(ex_b1[...], axis=0)
    gather(fu_b1, 18, PLANE, gp)
    arrive(20)
    fu_d1[gn, 0:16] = ex_d1[...]
    fu_d1[gn, 16:24] = red_d1[16:24]
    gather(fu_d1, 21, NODE, gn)
    arrive(14)
    fu_d0[gn, 0:16] = jnp.sum(ex_d0[...], axis=0)
    fu_d0[gn, 16:40] = red_d0[16:40]
    gather(fu_d0, 15, NODE, gn)
    basis[1] = thin(yref[...], g1)
    write(basis.at[1], basis_out.at[1], 1)
    split_sample(2)
    arrive(18)
    c1 = couple(s1, fu_b1[...].reshape(SAMPLES, SKEL))
    coup[1] = c1

    arrive(15)
    k2t = exact(fu_d0[:, 0:16].reshape(SAMPLES, SKEL), c0, TRANSPOSED)
    part2 = blocks_to_matrix(fu_d0[:, 24:40]) - exact(fu_d0[0:16, 16:24].reshape(SKEL, SKEL), k2t, TRANSPOSED)
    arrive(21)
    k3t = exact(fu_d1[:, 0:16].reshape(SAMPLES, SKEL), c1, TRANSPOSED)
    s2 = part2 - exact(fu_d1[0:16, 16:24].reshape(SKEL, SKEL), k3t, TRANSPOSED)
    y = project(2, s2) - thin(basis[0], exact(s2, k2t), TRANSPOSED) - thin(basis[1], exact(s2, k3t), TRANSPOSED)
    yref[...] = y
    yh, yl = split(y)
    ycat = jnp.concatenate([yh, yl], axis=1)
    st_b2[...] = test(2, yh, ycat).reshape(32, 16, 128)
    scatter(st_b2, rs_b2, 22, SIBLING, in_node)
    red_b2[...] = gram_inverse(s2)
    exchange([(red_b2, ex_b2, (4, 0))], ex_b2, 23)
    arrive(22)
    fu_b2[gn] = jnp.sum(rs_b2[...], axis=0)
    gather(fu_b2, 24, NODE, gn)
    basis[2] = thin(yref[...], red_b2[...])
    write(basis.at[2], basis_out.at[2], 2)
    arrive(23)
    arrive(24)
    coup[2] = couple(s2, exact(fu_b2[...].reshape(SAMPLES, SKEL), ex_b2[...]))
    write(coup, coupling_out, 3)

    finish()


def vm(*shape, dtype=F32):
    return pltpu.VMEM(shape, dtype)


def local(sample, probes, skeleton_rows):
    def phase(rows, ex, received=31):
        return [vm(32, rows, 128), vm(received, rows, 128), *ex, vm(32, rows, 128), vm(rows, 128)]

    scratch = [
        vm(ROWS, SAMPLES), vm(ROWS, SAMPLES), vm(ROWS, SAMPLES), vm(3, ROWS, SAMPLES),
        vm(3, ROWS, SAMPLES, dtype=BF16), vm(3, ROWS, SAMPLES, dtype=BF16),
        vm(3, SAMPLES, ROWS, dtype=BF16), vm(3, SAMPLES, ROWS, dtype=BF16),
        vm(ROWS, SKEL), vm(3, ROWS, SKEL), vm(3, SKEL, SKEL),
        *phase(16, [vm(3, 16, 128)]),
        *phase(16, [vm(16, 128)]),
        *phase(16, [vm(4, 16, 128)]),
        *phase(24, [vm(2, 16, 128), vm(8, 128)]),
        *phase(40, [vm(2, 16, 128)]),
        *phase(16, [vm(2, 16, 128)]),
        *phase(24, [vm(16, 128)]),
        vm(32, 16, 128), vm(32, 16, 128), vm(SKEL, SKEL), vm(32, 16, 128), vm(SKEL, SKEL),
        pltpu.SemaphoreType.DMA((25,)), pltpu.SemaphoreType.DMA((25,)),
        pltpu.SemaphoreType.DMA((6,)), pltpu.SemaphoreType.DMA((4,)),
    ]
    basis, coupling = pl.pallas_call(
        kernel,
        out_shape=(
            jax.ShapeDtypeStruct((3, ROWS, SKEL), F32),
            jax.ShapeDtypeStruct((3, SKEL, SKEL), F32),
        ),
        in_specs=[
            pl.BlockSpec(memory_space=pltpu.SMEM),
            pl.BlockSpec(memory_space=pl.ANY),
            pl.BlockSpec(memory_space=pl.ANY),
        ],
        out_specs=(pl.BlockSpec(memory_space=pl.ANY), pl.BlockSpec(memory_space=pl.ANY)),
        scratch_shapes=scratch,
        compiler_params=pltpu.CompilerParams(
            collective_id=0, has_side_effects=True, vmem_limit_bytes=52 * 2**20
        ),
    )(skeleton_rows, sample, probes)
    return basis, coupling[:, None]


def solution(mesh):
    placed = (P(None, ("leaf", "blk"), None), P(None, ("leaf", "blk"), None), P())
    return jax.shard_map(
        local,
        mesh=mesh,
        in_specs=placed,
        out_specs=(P(None, ("leaf", "blk"), None), P(None, "leaf", None, None)),
        check_vma=False,
    )
```

time: 129 us -> 114 us (0.88)
  Pallas kernels: 126 us -> 111 us
    pallas_call x1, Pallas kernels: 126 us -> 111 us  [local(): pl.pallas_call(kernel, out_shape=(jax.ShapeDtypeStruct((3, ROWS, SKEL), F...]
where the time goes in v2:
time: 114 us
  Pallas kernels  111 us (97%)
  local copies, waits for them, and re-layouts  2.45 us (2%)
    pallas_call x1, Pallas kernels, local(): pl.pallas_call(kernel, out_shape=(jax.ShapeDtypeStruct((3, ROWS, SKEL), F...  111 us
    unnamed x4, local copies, waits for them, and re-layouts  2.45 us

profile of v2, /device:TPU:1, one launch (start us, length us, event | category | flops | bytes accessed | tf_op | source)
XLA Modules:
  0.0 113.7 jit_solution(16122966174125608190)
XLA Ops:
  0.6 0.0 copy-start
  0.6 0.7 copy-done
  1.3 110.6 %shard_map.50 = (f32[3,896,128]{2,1,0:T(8,128)S(1)}, f32[3,128,128]{2,1,0:T(8,128)S(1)}) custom-call(s32[14,128]{1,0:T(8,128)S(1)} %copy-done, f32[3,896,512]{2,1,0:T(8,128)} %sample_ref.1, f32[3,896,512]{2,1,0:T(8,128)} %probes_ref.1), custom_call_target="tpu_custom_call" | custom-call | tf_op jit(solution)/shard_map/pallas_call | solution.py:420
  111.9 1.1 copy.8
  113.0 0.7 copy.9
Async XLA Ops:
  0.6 0.7 copy-start

commit v3 on v2

--- a/solution.py
+++ b/solution.py
@@ -17,8 +17,10 @@
 NROWS = 229376
 
 STEP = 16
+A0, A1, B0, C0, D0, B1, D1, B2 = range(0, 48, 6)
 
 HOPS = (0, 1, 2, 1)
+CORE = (1, 0)
 
 
 def far(mask):
@@ -26,18 +28,17 @@
     return HOPS[a >> 1 & 3] + HOPS[b & 3] + (b >> 2)
 
 
-def masks(first, leaf_bits, blk_bits):
-    every = [(first + a, b) for a in range(1 << leaf_bits) for b in range(1 << blk_bits)]
+def masks(leaf_masks, blk_masks):
+    every = [(a, b) for a in leaf_masks for b in range(blk_masks)]
     return tuple(sorted((m for m in every if m != (0, 0)), key=lambda m: -far(m)))
 
 
-NODE = masks(0, 2, 3)
-PLANE = masks(0, 3, 2)
-SIBLING = masks(4, 2, 3)
+NODE = masks((0, 2), 8)
+PLANE = masks((0, 2, 4, 6), 4)
+SIBLING = masks((4, 6), 8)
 HALF = ((0, 4), (8, 0), (8, 4))
 ACROSS = ((16, 0), (16, 4), (24, 0), (24, 4))
-OTHERS = HALF + ACROSS + ((20, 0), (28, 0), (12, 0))
-ALL = tuple(dict.fromkeys(SIBLING + NODE + PLANE + OTHERS))
+ALL = tuple(dict.fromkeys(ACROSS + ((12, 0),) + SIBLING + HALF + PLANE + NODE + (CORE,)))
 
 ROWMAJOR = (((1,), (0,)), ((), ()))
 TRANSPOSED = (((1,), (1,)), ((), ()))
@@ -94,14 +95,14 @@
 def kernel(
     rows_ref, sample_ref, probes_ref, basis_out, coupling_out,
     samp0, samp1, samp2, prob, sh, sl, pth, ptl, yref, basis, coup,
-    st_a0, rs_a0, ex_a0, fu_a0, red_a0,
-    st_a1, rs_a1, ex_a1, fu_a1, red_a1,
-    st_b0, rs_b0, ex_b0, fu_b0, red_b0,
-    st_c0, rs_c0, ex_c0, exy_c0, fu_c0, red_c0,
-    st_d0, rs_d0, ex_d0, fu_d0, red_d0,
-    st_b1, rs_b1, ex_b1, fu_b1, red_b1,
-    st_d1, rs_d1, ex_d1, fu_d1, red_d1,
-    st_b2, rs_b2, ex_b2, fu_b2, red_b2,
+    st_a0, co_a0, rs_a0, ex_a0, fu_a0, red_a0,
+    st_a1, co_a1, rs_a1, ex_a1, fu_a1, red_a1,
+    st_b0, co_b0, rs_b0, ex_b0, fu_b0, red_b0,
+    st_c0, co_c0, rs_c0, ex_c0, exy_c0, fu_c0, red_c0,
+    st_d0, co_d0, rs_d0, ex_d0, exy_d0, fu_d0, red_d0, swap_d0,
+    st_b1, co_b1, rs_b1, ex_b1, fu_b1, red_b1,
+    st_d1, co_d1, rs_d1, ex_d1, fu_d1, red_d1,
+    st_b2, co_b2, rs_b2, ex_b2, fu_b2, red_b2,
     ssem, rsem, insem, outsem,
 ):
     samp = (samp0, samp1, samp2)
@@ -120,11 +121,15 @@
                 b = b + blk_step[k]
         return a, b
 
+    core = leaf % 2
+    own = pl.ds(16 * core, 16)
+    other = pl.ds(16 * (1 - core), 16)
+
     def in_node(a, b):
-        return (a % 4) * 8 + b
+        return (a % 2) * 16 + (a // 2 % 2) * 8 + b
 
     def in_plane(a, b):
-        return (a % 8) * 4 + b % 4
+        return (a % 2) * 16 + (a // 2 % 4) * 4 + b % 4
 
     gn = in_node(leaf, blk)
     gp = in_plane(leaf, blk)
@@ -174,11 +179,17 @@
             device_id=to, device_id_type=MESH,
         ).start()
 
-    def scatter(st, rs, stage, group, number):
+    def share(st, co, stage):
+        send(st.at[other], co, stage, at(CORE))
+        start(co, stage)
+
+    def scatter(st, co, rs, stage, group, number):
+        arrive(stage)
+        st[own] = st[own] + co[...]
         for i, m in enumerate(group):
             to = at(m)
-            send(st.at[number(*to)], rs.at[i], stage, to)
-        start(rs, stage)
+            send(st.at[number(*to)], rs.at[i], stage + 1, to)
+        start(rs, stage + 1)
 
     def exchange(pieces, ex, stage):
         for src, dst, m in pieces:
@@ -188,14 +199,19 @@
     def gather(fu, stage, group, mine):
         for m in group:
             send(fu.at[mine], fu.at[mine], stage, at(m))
-        start(fu.at[pl.ds(1, 31)], stage)
+        start(fu.at[pl.ds(0, 15)], stage)
+
+    def forward(fu, stage):
+        arrive(stage)
+        send(fu.at[own], fu.at[own], stage + 1, at(CORE))
+        start(fu.at[other], stage + 1)
 
     def pick(level, base, table_row, source, put):
         def one(i, _):
             place = rows_ref[table_row, i] + base
-            own = (place >= 0) & (place < ROWS)
+            here = (place >= 0) & (place < ROWS)
             safe = jnp.clip(place, 0, ROWS - 1)
-            put(i, jnp.where(own, source(safe), 0.0))
+            put(i, jnp.where(here, source(safe), 0.0))
             return 0
 
         lax.fori_loop(0, SKEL, one, 0, unroll=8)
@@ -260,71 +276,82 @@
     loads.pop(0).wait()
     pick_sample(0, st_a0, 0)
     pl.semaphore_wait(barrier, len(ALL))
-    scatter(st_a0, rs_a0, 0, PLANE, in_plane)
+    share(st_a0, co_a0, A0)
     loads.pop(1).wait()
+    scatter(st_a0, co_a0, rs_a0, A0, PLANE, in_plane)
     pick_sample(1, st_a1, 0)
-    scatter(st_a1, rs_a1, 3, PLANE, in_plane)
+    share(st_a1, co_a1, A1)
     split_sample(0)
-    arrive(0)
+    scatter(st_a1, co_a1, rs_a1, A1, PLANE, in_plane)
+    arrive(A0 + 1)
     red_a0[...] = st_a0[gp] + jnp.sum(rs_a0[...], axis=0)
-    exchange([(red_a0, ex_a0.at[i], m) for i, m in enumerate(HALF)], ex_a0, 1)
+    exchange([(red_a0, ex_a0.at[i], m) for i, m in enumerate(HALF)], ex_a0, A0 + 2)
     loads.pop(3).wait()
     split_probes(0)
-    arrive(3)
+    arrive(A0 + 2)
+    fu_a0[gp] = red_a0[...] + jnp.sum(ex_a0[...], axis=0)
+    gather(fu_a0, A0 + 3, PLANE, gp)
+    arrive(A1 + 1)
     red_a1[...] = st_a1[gp] + jnp.sum(rs_a1[...], axis=0)
-    arrive(1)
-    fu_a0[gp] = red_a0[...] + jnp.sum(ex_a0[...], axis=0)
-    gather(fu_a0, 2, PLANE, gp)
-    exchange([(red_a1, ex_a1, (0, 4))], ex_a1, 4)
+    exchange([(red_a1, ex_a1, (0, 4))], ex_a1, A1 + 2)
+    loads.pop(4).wait()
+    split_probes(1)
     loads.pop(2).wait()
     pick_sample(2, st_d0, 24)
-    loads.pop(4).wait()
-    split_probes(1)
-    loads.pop(5).wait()
-    split_probes(2)
-    arrive(4)
+    forward(fu_a0, A0 + 3)
+    arrive(A1 + 2)
     fu_a1[gp] = red_a1[...] + ex_a1[...]
-    gather(fu_a1, 5, PLANE, gp)
-
-    arrive(2)
+    gather(fu_a1, A1 + 3, PLANE, gp)
+    arrive(A0 + 4)
+
     s0 = blocks_to_matrix(fu_a0)
     y = project(0, s0)
     yref[...] = y
     yh, yl = split(y)
     ycat = jnp.concatenate([yh, yl], axis=1)
     st_b0[...] = test(0, yh, ycat).reshape(32, 16, 128)
-    scatter(st_b0, rs_b0, 6, PLANE, in_plane)
+    share(st_b0, co_b0, B0)
     st_c0[:, 0:16] = test(1, yh, ycat).reshape(32, 16, 128)
     pick_y(1, st_c0, 16)
-    scatter(st_c0, rs_c0, 9, PLANE, in_plane)
+    scatter(st_b0, co_b0, rs_b0, B0, PLANE, in_plane)
+    share(st_c0, co_c0, C0)
+    forward(fu_a1, A1 + 3)
+    loads.pop(5).wait()
+    split_probes(2)
+    scatter(st_c0, co_c0, rs_c0, C0, PLANE, in_plane)
     g0 = gram_inverse(s0)
-    arrive(6)
+    arrive(B0 + 1)
     red_b0[...] = exact(st_b0[gp] + jnp.sum(rs_b0[...], axis=0), g0)
-    exchange([(red_b0, ex_b0.at[i], m) for i, m in enumerate(ACROSS)], ex_b0, 7)
-    arrive(9)
+    exchange([(red_b0, ex_b0.at[i], m) for i, m in enumerate(ACROSS)], ex_b0, B0 + 2)
+    arrive(C0 + 1)
     red_c0[...] = exact(st_c0[gp] + jnp.sum(rs_c0[...], axis=0), g0)
-    exchange([(red_c0.at[pl.ds(0, 16)], ex_c0.at[i], m) for i, m in enumerate(ACROSS[2:])], ex_c0, 10)
-    exchange([(red_c0.at[pl.ds(16, 8)], exy_c0, (0, 4))], exy_c0, 11)
-    st_d0[:, 0:16] = test(2, yh, ycat).reshape(32, 16, 128)
+    exchange([(red_c0.at[pl.ds(0, 16)], ex_c0.at[i], m) for i, m in enumerate(ACROSS[2:])], ex_c0, C0 + 2)
+    exchange([(red_c0.at[pl.ds(16, 8)], exy_c0, (0, 4))], exy_c0, C0 + 5)
+    yh, yl = split(yref[...])
+    st_d0[:, 0:16] = test(2, yh, jnp.concatenate([yh, yl], axis=1)).reshape(32, 16, 128)
     pick_y(2, st_d0, 16)
-    arrive(7)
+    share(st_d0, co_d0, D0)
+    arrive(B0 + 2)
     fu_b0[gp] = jnp.sum(ex_b0[...], axis=0)
-    gather(fu_b0, 8, PLANE, gp)
-    arrive(10)
-    arrive(11)
+    gather(fu_b0, B0 + 3, PLANE, gp)
+    arrive(C0 + 2)
+    arrive(C0 + 5)
     fu_c0[gp, 0:16] = jnp.sum(ex_c0[...], axis=0)
     fu_c0[gp, 16:24] = red_c0[16:24] + exy_c0[...]
-    gather(fu_c0, 12, PLANE, gp)
+    gather(fu_c0, C0 + 3, PLANE, gp)
     basis[0] = thin(yref[...], g0)
     write(basis.at[0], basis_out.at[0], 0)
     split_sample(1)
-    arrive(8)
-    scatter(st_d0, rs_d0, 13, NODE, in_node)
-    c0 = couple(s0, fu_b0[...].reshape(SAMPLES, SKEL))
+    forward(fu_b0, B0 + 3)
+    scatter(st_d0, co_d0, rs_d0, D0, NODE, in_node)
+    arrive(B0 + 4)
+    m0 = fu_b0[...].reshape(SAMPLES, SKEL)
+    forward(fu_c0, C0 + 3)
+    c0 = couple(s0, m0)
     coup[0] = c0
 
-    arrive(5)
-    arrive(12)
+    arrive(A1 + 4)
+    arrive(C0 + 4)
     k1t = exact(fu_c0[:, 0:16].reshape(SAMPLES, SKEL), c0, TRANSPOSED)
     s1 = blocks_to_matrix(fu_a1) - exact(fu_c0[0:16, 16:24].reshape(SKEL, SKEL), k1t, TRANSPOSED)
     y = project(1, s1) - thin(basis[0], exact(s1, k1t), TRANSPOSED)
@@ -332,44 +359,53 @@
     yh, yl = split(y)
     ycat = jnp.concatenate([yh, yl], axis=1)
     st_b1[...] = test(1, yh, ycat).reshape(32, 16, 128)
-    scatter(st_b1, rs_b1, 16, PLANE, in_plane)
+    share(st_b1, co_b1, B1)
     st_d1[:, 0:16] = test(2, yh, ycat).reshape(32, 16, 128)
     pick_y(2, st_d1, 16)
-    scatter(st_d1, rs_d1, 19, NODE, in_node)
-    arrive(13)
+    scatter(st_b1, co_b1, rs_b1, B1, PLANE, in_plane)
+    share(st_d1, co_d1, D1)
+    arrive(D0 + 1)
     sum_d0 = st_d0[gn] + jnp.sum(rs_d0[...], axis=0)
     red_d0[0:24] = exact(sum_d0[0:24], g0)
     red_d0[24:40] = sum_d0[24:40]
-    exchange([(red_d0.at[pl.ds(0, 16)], ex_d0.at[i], m) for i, m in enumerate(((20, 0), (28, 0)))], ex_d0, 14)
+    exchange([(red_d0.at[pl.ds(0, 16)], ex_d0.at[i], m) for i, m in enumerate(((16, 0), (24, 0)))], ex_d0, D0 + 2)
+    scatter(st_d1, co_d1, rs_d1, D1, NODE, in_node)
     g1 = gram_inverse(s1)
-    arrive(16)
+    arrive(B1 + 1)
     red_b1[...] = exact(st_b1[gp] + jnp.sum(rs_b1[...], axis=0), g1)
-    exchange([(red_b1, ex_b1.at[i], m) for i, m in enumerate(((8, 0), (8, 4)))], ex_b1, 17)
-    arrive(19)
+    exchange([(red_b1, ex_b1.at[i], m) for i, m in enumerate(((8, 0), (8, 4)))], ex_b1, B1 + 2)
+    arrive(D1 + 1)
     red_d1[...] = exact(st_d1[gn] + jnp.sum(rs_d1[...], axis=0), g1)
-    exchange([(red_d1.at[pl.ds(0, 16)], ex_d1, (12, 0))], ex_d1, 20)
-    arrive(17)
+    exchange([(red_d1.at[pl.ds(0, 16)], ex_d1, (12, 0))], ex_d1, D1 + 2)
+    arrive(D0 + 2)
+    swap_d0[...] = jnp.sum(ex_d0[...], axis=0)
+    exchange([(swap_d0, exy_d0, (4, 0))], exy_d0, D0 + 5)
+    arrive(B1 + 2)
     fu_b1[gp] = jnp.sum(ex_b1[...], axis=0)
-    gather(fu_b1, 18, PLANE, gp)
-    arrive(20)
+    gather(fu_b1, B1 + 3, PLANE, gp)
+    arrive(D0 + 5)
+    fu_d0[gn, 0:16] = exy_d0[...]
+    fu_d0[gn, 16:40] = red_d0[16:40]
+    gather(fu_d0, D0 + 3, NODE, gn)
+    arrive(D1 + 2)
     fu_d1[gn, 0:16] = ex_d1[...]
     fu_d1[gn, 16:24] = red_d1[16:24]
-    gather(fu_d1, 21, NODE, gn)
-    arrive(14)
-    fu_d0[gn, 0:16] = jnp.sum(ex_d0[...], axis=0)
-    fu_d0[gn, 16:40] = red_d0[16:40]
-    gather(fu_d0, 15, NODE, gn)
+    gather(fu_d1, D1 + 3, NODE, gn)
     basis[1] = thin(yref[...], g1)
     write(basis.at[1], basis_out.at[1], 1)
     split_sample(2)
-    arrive(18)
-    c1 = couple(s1, fu_b1[...].reshape(SAMPLES, SKEL))
+    forward(fu_b1, B1 + 3)
+    arrive(B1 + 4)
+    m1 = fu_b1[...].reshape(SAMPLES, SKEL)
+    forward(fu_d0, D0 + 3)
+    forward(fu_d1, D1 + 3)
+    c1 = couple(s1, m1)
     coup[1] = c1
 
-    arrive(15)
+    arrive(D0 + 4)
     k2t = exact(fu_d0[:, 0:16].reshape(SAMPLES, SKEL), c0, TRANSPOSED)
     part2 = blocks_to_matrix(fu_d0[:, 24:40]) - exact(fu_d0[0:16, 16:24].reshape(SKEL, SKEL), k2t, TRANSPOSED)
-    arrive(21)
+    arrive(D1 + 4)
     k3t = exact(fu_d1[:, 0:16].reshape(SAMPLES, SKEL), c1, TRANSPOSED)
     s2 = part2 - exact(fu_d1[0:16, 16:24].reshape(SKEL, SKEL), k3t, TRANSPOSED)
     y = project(2, s2) - thin(basis[0], exact(s2, k2t), TRANSPOSED) - thin(basis[1], exact(s2, k3t), TRANSPOSED)
@@ -377,16 +413,19 @@
     yh, yl = split(y)
     ycat = jnp.concatenate([yh, yl], axis=1)
     st_b2[...] = test(2, yh, ycat).reshape(32, 16, 128)
-    scatter(st_b2, rs_b2, 22, SIBLING, in_node)
-    red_b2[...] = gram_inverse(s2)
-    exchange([(red_b2, ex_b2, (4, 0))], ex_b2, 23)
-    arrive(22)
+    share(st_b2, co_b2, B2)
+    gram = with_ridge(exact(s2, s2, TRANSPOSED), SAMPLES * RIDGE)
+    scatter(st_b2, co_b2, rs_b2, B2, SIBLING, in_node)
+    red_b2[...] = inverse(gram)
+    exchange([(red_b2, ex_b2, (4, 0))], ex_b2, B2 + 2)
+    arrive(B2 + 1)
     fu_b2[gn] = jnp.sum(rs_b2[...], axis=0)
-    gather(fu_b2, 24, NODE, gn)
+    gather(fu_b2, B2 + 3, NODE, gn)
     basis[2] = thin(yref[...], red_b2[...])
     write(basis.at[2], basis_out.at[2], 2)
-    arrive(23)
-    arrive(24)
+    forward(fu_b2, B2 + 3)
+    arrive(B2 + 2)
+    arrive(B2 + 4)
     coup[2] = couple(s2, exact(fu_b2[...].reshape(SAMPLES, SKEL), ex_b2[...]))
     write(coup, coupling_out, 3)
 
@@ -398,8 +437,10 @@
 
 
 def local(sample, probes, skeleton_rows):
-    def phase(rows, ex, received=31):
-        return [vm(32, rows, 128), vm(received, rows, 128), *ex, vm(32, rows, 128), vm(rows, 128)]
+    def phase(rows, ex, received=15):
+        return [
+            vm(32, rows, 128), vm(16, rows, 128), vm(received, rows, 128), *ex, vm(32, rows, 128), vm(rows, 128),
+        ]
 
     scratch = [
         vm(ROWS, SAMPLES), vm(ROWS, SAMPLES), vm(ROWS, SAMPLES), vm(3, ROWS, SAMPLES),
@@ -410,11 +451,11 @@
         *phase(16, [vm(16, 128)]),
         *phase(16, [vm(4, 16, 128)]),
         *phase(24, [vm(2, 16, 128), vm(8, 128)]),
-        *phase(40, [vm(2, 16, 128)]),
+        *phase(40, [vm(2, 16, 128), vm(16, 128)]), vm(16, 128),
         *phase(16, [vm(2, 16, 128)]),
         *phase(24, [vm(16, 128)]),
-        vm(32, 16, 128), vm(32, 16, 128), vm(SKEL, SKEL), vm(32, 16, 128), vm(SKEL, SKEL),
-        pltpu.SemaphoreType.DMA((25,)), pltpu.SemaphoreType.DMA((25,)),
+        vm(32, 16, 128), vm(16, 16, 128), vm(16, 16, 128), vm(SKEL, SKEL), vm(32, 16, 128), vm(SKEL, SKEL),
+        pltpu.SemaphoreType.DMA((48,)), pltpu.SemaphoreType.DMA((48,)),
         pltpu.SemaphoreType.DMA((6,)), pltpu.SemaphoreType.DMA((4,)),
     ]
     basis, coupling = pl.pallas_call(

time: 114 us -> 108 us (0.947)
  Pallas kernels: 111 us -> 104 us
    pallas_call x1, Pallas kernels: 111 us -> 104 us  [local(): pl.pallas_call(kernel, out_shape=(jax.ShapeDtypeStruct((3, ROWS, SKEL), F...]
where the time goes in v3:
time: 108 us
  Pallas kernels  104 us (96%)
  local copies, waits for them, and re-layouts  2.45 us (2%)
    pallas_call x1, Pallas kernels, local(): pl.pallas_call(kernel, out_shape=(jax.ShapeDtypeStruct((3, ROWS, SKEL), F...  104 us
    unnamed x4, local copies, waits for them, and re-layouts  2.45 us

profile of v3, /device:TPU:1, one launch (start us, length us, event | category | flops | bytes accessed | tf_op | source)
XLA Modules:
  0.0 107.6 jit_solution(6997640988163731317)
XLA Ops:
  0.6 0.0 copy-start
  0.6 0.7 copy-done
  1.3 104.5 %shard_map.50 = (f32[3,896,128]{2,1,0:T(8,128)S(1)}, f32[3,128,128]{2,1,0:T(8,128)S(1)}) custom-call(s32[14,128]{1,0:T(8,128)S(1)} %copy-done, f32[3,896,512]{2,1,0:T(8,128)} %sample_ref.1, f32[3,896,512]{2,1,0:T(8,128)} %probes_ref.1), custom_call_target="tpu_custom_call" | custom-call | tf_op jit(solution)/shard_map/pallas_call | solution.py:461
  105.8 1.1 %copy.8 = f32[3,896,128]{2,1,0:T(8,128)} copy(f32[3,896,128]{2,1,0:T(8,128)S(1)} %get-tuple-element.10) | data formatting | bytes 2752512
  106.9 0.7 copy.9
Async XLA Ops:
  0.6 0.7 copy-start

commit v4 on v3

--- a/solution.py
+++ b/solution.py
@@ -57,7 +57,7 @@
     return lax.dot_general(a, b, dims, precision=lax.Precision.HIGHEST, preferred_element_type=F32)
 
 
-def inverse(a):
+def inverse(a, halfway=None):
     lane = lax.broadcasted_iota(jnp.int32, (STEP, 128), 1)
     sub = lax.broadcasted_iota(jnp.int32, (STEP, 128), 0)
     lane_rest = lax.broadcasted_iota(jnp.int32, (128 - STEP, 128), 1)
@@ -79,7 +79,10 @@
             n = n - r[:, i : i + 1] * p[i : i + 1]
         return pltpu.roll(jnp.concatenate([n, p], 0), 128 - STEP, 1)
 
-    return lax.fori_loop(0, 128 // STEP, body, a)
+    a = lax.fori_loop(0, 64 // STEP, body, a)
+    if halfway:
+        halfway()
+    return lax.fori_loop(0, 64 // STEP, body, a)
 
 
 def with_ridge(a, ridge):
@@ -265,13 +268,13 @@
         bh, bl = split(b)
         return dot(ah, bh, dims) + dot(ah, bl, dims) + dot(al, bh, dims)
 
-    def couple(s, mt):
+    def couple(s, mt, halfway=None):
         m = mt.T
-        spread = inverse(with_ridge(exact(m, m, TRANSPOSED), RIDGE))
+        spread = inverse(with_ridge(exact(m, m, TRANSPOSED), RIDGE), halfway)
         return exact(exact(s, mt), spread)
 
-    def gram_inverse(s):
-        return inverse(with_ridge(exact(s, s, TRANSPOSED), SAMPLES * RIDGE))
+    def gram_inverse(s, halfway=None):
+        return inverse(with_ridge(exact(s, s, TRANSPOSED), SAMPLES * RIDGE), halfway)
 
     loads.pop(0).wait()
     pick_sample(0, st_a0, 0)
@@ -298,6 +301,8 @@
     split_probes(1)
     loads.pop(2).wait()
     pick_sample(2, st_d0, 24)
+    loads.pop(5).wait()
+    split_probes(2)
     forward(fu_a0, A0 + 3)
     arrive(A1 + 2)
     fu_a1[gp] = red_a1[...] + ex_a1[...]
@@ -315,11 +320,8 @@
     pick_y(1, st_c0, 16)
     scatter(st_b0, co_b0, rs_b0, B0, PLANE, in_plane)
     share(st_c0, co_c0, C0)
-    forward(fu_a1, A1 + 3)
-    loads.pop(5).wait()
-    split_probes(2)
     scatter(st_c0, co_c0, rs_c0, C0, PLANE, in_plane)
-    g0 = gram_inverse(s0)
+    g0 = gram_inverse(s0, lambda: forward(fu_a1, A1 + 3))
     arrive(B0 + 1)
     red_b0[...] = exact(st_b0[gp] + jnp.sum(rs_b0[...], axis=0), g0)
     exchange([(red_b0, ex_b0.at[i], m) for i, m in enumerate(ACROSS)], ex_b0, B0 + 2)
@@ -346,8 +348,7 @@
     scatter(st_d0, co_d0, rs_d0, D0, NODE, in_node)
     arrive(B0 + 4)
     m0 = fu_b0[...].reshape(SAMPLES, SKEL)
-    forward(fu_c0, C0 + 3)
-    c0 = couple(s0, m0)
+    c0 = couple(s0, m0, lambda: forward(fu_c0, C0 + 3))
     coup[0] = c0
 
     arrive(A1 + 4)
@@ -370,23 +371,26 @@
     red_d0[24:40] = sum_d0[24:40]
     exchange([(red_d0.at[pl.ds(0, 16)], ex_d0.at[i], m) for i, m in enumerate(((16, 0), (24, 0)))], ex_d0, D0 + 2)
     scatter(st_d1, co_d1, rs_d1, D1, NODE, in_node)
-    g1 = gram_inverse(s1)
+
+    def swap():
+        arrive(D0 + 2)
+        swap_d0[...] = jnp.sum(ex_d0[...], axis=0)
+        exchange([(swap_d0, exy_d0, (4, 0))], exy_d0, D0 + 5)
+
+    g1 = gram_inverse(s1, swap)
     arrive(B1 + 1)
     red_b1[...] = exact(st_b1[gp] + jnp.sum(rs_b1[...], axis=0), g1)
     exchange([(red_b1, ex_b1.at[i], m) for i, m in enumerate(((8, 0), (8, 4)))], ex_b1, B1 + 2)
-    arrive(D1 + 1)
-    red_d1[...] = exact(st_d1[gn] + jnp.sum(rs_d1[...], axis=0), g1)
-    exchange([(red_d1.at[pl.ds(0, 16)], ex_d1, (12, 0))], ex_d1, D1 + 2)
-    arrive(D0 + 2)
-    swap_d0[...] = jnp.sum(ex_d0[...], axis=0)
-    exchange([(swap_d0, exy_d0, (4, 0))], exy_d0, D0 + 5)
-    arrive(B1 + 2)
-    fu_b1[gp] = jnp.sum(ex_b1[...], axis=0)
-    gather(fu_b1, B1 + 3, PLANE, gp)
     arrive(D0 + 5)
     fu_d0[gn, 0:16] = exy_d0[...]
     fu_d0[gn, 16:40] = red_d0[16:40]
     gather(fu_d0, D0 + 3, NODE, gn)
+    arrive(D1 + 1)
+    red_d1[...] = exact(st_d1[gn] + jnp.sum(rs_d1[...], axis=0), g1)
+    exchange([(red_d1.at[pl.ds(0, 16)], ex_d1, (12, 0))], ex_d1, D1 + 2)
+    arrive(B1 + 2)
+    fu_b1[gp] = jnp.sum(ex_b1[...], axis=0)
+    gather(fu_b1, B1 + 3, PLANE, gp)
     arrive(D1 + 2)
     fu_d1[gn, 0:16] = ex_d1[...]
     fu_d1[gn, 16:24] = red_d1[16:24]
@@ -398,8 +402,7 @@
     arrive(B1 + 4)
     m1 = fu_b1[...].reshape(SAMPLES, SKEL)
     forward(fu_d0, D0 + 3)
-    forward(fu_d1, D1 + 3)
-    c1 = couple(s1, m1)
+    c1 = couple(s1, m1, lambda: forward(fu_d1, D1 + 3))
     coup[1] = c1
 
     arrive(D0 + 4)

time: 108 us -> 106 us (0.981)
    pallas_call x1, Pallas kernels: 104 us -> 103 us  [local(): pl.pallas_call(kernel, out_shape=(jax.ShapeDtypeStruct((3, ROWS, SKEL), F...]
where the time goes in v4:
time: 106 us
  Pallas kernels  103 us (97%)
  local copies, waits for them, and re-layouts  2.45 us (2%)
    pallas_call x1, Pallas kernels, local(): pl.pallas_call(kernel, out_shape=(jax.ShapeDtypeStruct((3, ROWS, SKEL), F...  103 us
    unnamed x4, local copies, waits for them, and re-layouts  2.45 us

profile of v4, /device:TPU:1, one launch (start us, length us, event | category | flops | bytes accessed | tf_op | source)
XLA Modules:
  0.0 105.7 jit_solution(7504244535210658675)
XLA Ops:
  0.6 0.0 copy-start
  0.6 0.7 copy-done
  1.3 102.6 %shard_map.50 = (f32[3,896,128]{2,1,0:T(8,128)S(1)}, f32[3,128,128]{2,1,0:T(8,128)S(1)}) custom-call(s32[14,128]{1,0:T(8,128)S(1)} %copy-done, f32[3,896,512]{2,1,0:T(8,128)} %sample_ref.1, f32[3,896,512]{2,1,0:T(8,128)} %probes_ref.1), custom_call_target="tpu_custom_call" | custom-call | tf_op jit(solution)/shard_map/pallas_call | solution.py:464
  103.9 1.1 %copy.8 = f32[3,896,128]{2,1,0:T(8,128)} copy(f32[3,896,128]{2,1,0:T(8,128)S(1)} %get-tuple-element.10) | data formatting | bytes 2752512
  105.0 0.7 copy.9
Async XLA Ops:
  0.6 0.7 copy-start
